TPU v7x, 128 devices: a whole 4x4x4 slice. The times are simulated.
128 devices in a mesh: gx: 4 (over x), gy: 2 (over core), gz: 16 (over z, y).
Axes of the slice: x: 4, y: 4, z: 4, core: 2. Of those that a mesh axis runs over, the one named last changes fastest.
Arguments:
- x_in: bfloat16 [64, 256, 6144], P(('gy', 'gz'), None, 'gx'), may hold values from -64 to 64, as said below
- ln_gain: float32 [6144], P('gx'), may hold values from 0.25 to 1.75
- w_qkv: bfloat16 [6144, 24, 3, 128], P('gx', 'gy'), may hold values from -0.078125 to 0.078125
- q_gain: float32 [128], replicated, may hold values from 0.25 to 1.75
- k_gain: float32 [128], replicated, may hold values from 0.25 to 1.75
- w_out: bfloat16 [24, 128, 6144], P('gy', None, 'gx'), may hold values from -1.5 to 1.5
- counts: int32 [64, 8], P(('gy', 'gz')), may hold values from 1 to 64, 256 in all within a row
- dest: int32 [64, 8], P(('gy', 'gz')), may hold values from 0 to 15, as said below
Outputs:
- routed: bfloat16 [2, 16, 16, 1, 64, 6144], P('gy', 'gz', None, None, None, 'gx')
Inputs may be any that keep to these rules, and one draw needn't show every extreme that they name: x_in is of order one with row and feature scales of a factor up to ten. The 8 counts of an image sum to 256; the largest of them is exactly 64. `dest`: an image's 8 pieces go to different ranks; among the 2 images of one device (aligned blocks of rows) every rank is named exactly 1 times.
All inputs are finite; a program needn't handle non-finite values.
Results may differ from a plain program's by a relative error of at most 0.025.
Values may be sent and summed in bfloat16 or wider, within the bound.
A program may use at most 128 MiB of HBM per device.

v0:
```python
import math

import jax
import jax.numpy as jnp
from jax import lax
from jax.sharding import PartitionSpec as P

D = 6144


def normalize(values, total, squares, gain):
    mean_value = total[..., None] / D
    spread = squares[..., None] / D - mean_value * mean_value
    return (values - mean_value) * lax.rsqrt(spread + 1e-06) * gain


def head_norm(values, gain):
    mean_value = jnp.mean(values, axis=-1, keepdims=True)
    spread = jnp.mean(values * values, axis=-1, keepdims=True) - mean_value * mean_value
    return (values - mean_value) * lax.rsqrt(spread + 1e-06) * gain


def piece_slots(dest, counts, ranks, most, cap, patches):
    images, pieces = dest.shape
    total = images * pieces
    flat_dest = dest.reshape(total)
    flat_count = counts.reshape(total)
    offsets = (jnp.cumsum(counts, axis=1) - counts).reshape(total)
    order = jnp.arange(total, dtype=jnp.int32)
    image_of = order // pieces
    earlier = (flat_dest[None, :] == flat_dest[:, None]) & (order[None, :] < order[:, None])
    slot = jnp.sum(earlier.astype(jnp.int32), axis=1)
    rank_ids = jnp.arange(ranks, dtype=jnp.int32)
    slot_ids = jnp.arange(most, dtype=jnp.int32)
    select = (
        (flat_dest[None, None, :] == rank_ids[:, None, None])
        & (slot[None, None, :] == slot_ids[None, :, None])
    ).astype(jnp.int32)
    first = jnp.sum(select * (image_of * patches + offsets)[None, None, :], axis=2)
    length = jnp.sum(select * flat_count[None, None, :], axis=2)
    within = jnp.arange(cap, dtype=jnp.int32)
    valid = within[None, None, :] < length[:, :, None]
    index = jnp.where(valid, first[:, :, None] + within[None, None, :], 0)
    return (index, valid)


def on_device(x_in, ln_gain, w_qkv, q_gain, k_gain, w_out, counts, dest):
    images, patches, width = x_in.shape
    ranks = lax.axis_size("gz")
    xf = x_in.astype(jnp.float32)
    total, squares = lax.psum((jnp.sum(xf, axis=-1), jnp.sum(xf * xf, axis=-1)), "gx")
    normed = normalize(xf, total, squares, ln_gain).astype(jnp.bfloat16)
    gathered = lax.all_gather(normed, "gy", axis=0, tiled=True)
    rows_all = gathered.reshape(-1, width)
    heads_here = w_qkv.shape[1]
    head_dim = w_qkv.shape[3]
    qkv_mat = w_qkv.reshape(width, heads_here * 3 * head_dim)
    keep = rows_all.shape[0] // lax.axis_size("gx")
    qkv = lax.psum_scatter(
        jnp.dot(rows_all, qkv_mat, preferred_element_type=jnp.float32).astype(jnp.bfloat16),
        "gx",
        scatter_dimension=0,
        tiled=True,
    ).astype(jnp.float32)
    qkv = qkv.reshape(keep // patches, patches, heads_here, 3, head_dim)
    query = head_norm(qkv[:, :, :, 0, :], q_gain).astype(jnp.bfloat16)
    keys = head_norm(qkv[:, :, :, 1, :], k_gain).astype(jnp.bfloat16)
    values = qkv[:, :, :, 2, :].astype(jnp.bfloat16)
    scores = jnp.einsum(
        "iphe,ishe->ihps", query, keys, preferred_element_type=jnp.float32
    ) / math.sqrt(head_dim)
    expo = jnp.exp(scores)
    weights = (expo / jnp.sum(expo, axis=-1, keepdims=True)).astype(jnp.bfloat16)
    attended = jnp.einsum(
        "ihps,ishe->iphe", weights, values, preferred_element_type=jnp.float32
    ).astype(jnp.bfloat16)
    attended = attended.reshape(keep // patches, patches, heads_here * head_dim)
    head_rows = lax.all_gather(attended, "gx", axis=0, tiled=True)
    flat_heads = head_rows.reshape(-1, heads_here * head_dim)
    out_mat = w_out.reshape(heads_here * head_dim, width)
    projected = lax.psum_scatter(
        jnp.dot(flat_heads, out_mat, preferred_element_type=jnp.float32).astype(jnp.bfloat16),
        "gy",
        scatter_dimension=0,
        tiled=True,
    ).astype(jnp.float32)
    layer_out = (xf.reshape(images * patches, width) + projected).astype(jnp.bfloat16)
    pieces = dest.shape[1]
    most = images * pieces // ranks
    cap = 2 * patches // pieces
    index, valid = piece_slots(dest, counts, ranks, most, cap, patches)
    outgoing = jnp.take(layer_out, index.reshape(-1), axis=0).reshape(ranks, most, cap, width)
    outgoing = jnp.where(valid[:, :, :, None], outgoing, jnp.zeros((), jnp.bfloat16))
    received = lax.all_to_all(outgoing, "gz", split_axis=0, concat_axis=0, tiled=True)
    return received.reshape(1, 1, ranks, most, cap, width)


def solution(mesh):
    in_specs = (
        P(("gy", "gz"), None, "gx"),
        P("gx"),
        P("gx", "gy", None, None),
        P(),
        P(),
        P("gy", None, "gx"),
        P(("gy", "gz"), None),
        P(("gy", "gz"), None),
    )
    out_specs = P("gy", "gz", None, None, None, "gx")
    return jax.shard_map(
        on_device, mesh=mesh, in_specs=in_specs, out_specs=out_specs, check_vma=False
    )
```

profile of v0, /device:TPU:1, one launch (start us, length us, event | category | flops | bytes accessed | tf_op | source)
XLA Modules:
  0.0 284.7 jit_solution(13892600416640004643)
XLA Ops:
  6.5 2.0 convert_reduce_fusion
  8.5 9.3 %all-reduce = (f32[2,256]{1,0:T(2,128)S(1)}, f32[2,256]{1,0:T(2,128)S(1)}) all-reduce(f32[2,256]{1,0:T(2,128)S(1)} %get-tuple-element.10, f32[2,256]{1,0:T(2,128)S(1)} %get-tuple-element.9), channel_id=1, replica_groups=mesh['gx'=4,'gy'=2,'gz'=16] {'gx'}, use_global_device_ids=true, to_apply=%region_7.0 | all-reduce | flops 1024 | bytes 8192 | tf_op jit(solution)/shard_map/psum | solution.py:51
  17.8 3.1 %multiply_convert_fusion = bf16[2,256,1536]{2,1,0:T(8,128)(2,1)} fusion(bf16[2,256,1536]{2,1,0:T(8,128)(2,1)} %param.8, f32[1536]{0:T(1024)} %param.9, f32[2,256]{1,0:T(2,128)S(1)} %get-tuple-element.20, f32[2,256]{1,0:T(2,128)S(1)} %get-tuple-element.19), kind=kLoop, calls=%fused_computation.8 | loop fusion | flops 3932160 | bytes 3155968 | tf_op jit(solution)/shard_map/convert_element_type | solution.py:52
  21.0 18.9 %copy.28 = bf16[1536,12,3,128]{0,3,2,1:T(8,128)(2,1)} copy(bf16[1536,12,3,128]{3,0,2,1:T(8,128)(2,1)} %param.10) | data formatting | bytes 28311552 | tf_op args[2]
  39.9 20.2 %convolution_convert_fusion = bf16[1024,4608]{1,0:T(8,128)(2,1)} fusion(bf16[1024,1536]{1,0:T(8,128)(2,1)} %bitcast.60, bf16[1536,4608]{0,1:T(8,128)(2,1)} %bitcast.52), kind=kOutput, calls=%fused_computation.1 | convolution fusion | flops 14500233216 | bytes 26738688 | tf_op jit(solution)/shard_map/dot_general | solution.py:60
  60.1 91.2 %reduce-scatter.3.cloned.1.call-done = bf16[256,4608]{1,0:T(8,128)(2,1)} async-done(((bf16[1024,4608]{1,0:T(8,128)(2,1)}), bf16[256,4608]{1,0:T(8,128)(2,1)}) %reduce-scatter.3.cloned.1.call-update) | async-done | bytes 2359312 | tf_op jit(solution)/shard_map/reduce_scatter | solution.py:59
  151.3 2.8 copy.29
  154.2 0.6 reshape.510
  154.8 0.4 slice_reduce_fusion.1
  155.2 0.2 copy-done.2
  155.4 1.0 fusion.1
  156.4 0.7 fusion.9
  157.2 1.2 copy.34
  158.4 39.3 %all-gather.5.cloned.1.call-done = bf16[4,256,1536]{2,1,0:T(8,128)(2,1)} async-done(((bf16[1,256,1536]{2,1,0:T(8,128)(2,1)}), bf16[4,256,1536]{2,1,0:T(8,128)(2,1)}) %all-gather.5.cloned.1.call-update) | async-done | bytes 3145744 | tf_op jit(solution)/shard_map/all_gather | solution.py:78
  197.7 9.2 %convolution_convert_fusion.1 = bf16[1024,1536]{1,0:T(8,128)(2,1)} fusion(bf16[1024,1536]{1,0:T(8,128)(2,1)} %bitcast.61, bf16[1536,1536]{1,0:T(8,128)(2,1)} %bitcast.59), kind=kOutput, calls=%fused_computation.2 | convolution fusion | flops 4833411072 | bytes 11010048 | tf_op jit(solution)/shard_map/dot_general | solution.py:82
  206.9 0.6 copy-done.4
  207.8 0.2 reduce_window_sum.11
  208.0 0.2 convert_reduce_fusion.1
  208.6 12.6 %reduce-scatter.5.cloned.1.call-done = bf16[512,1536]{1,0:T(8,128)(2,1)} async-done(((bf16[1024,1536]{1,0:T(8,128)(2,1)}), bf16[512,1536]{1,0:T(8,128)(2,1)}) %reduce-scatter.5.cloned.1.call-update) | async-done | bytes 1572880 | tf_op jit(solution)/shard_map/reduce_scatter | solution.py:81
  221.3 1.8 fusion
  223.1 5.6 %gather_fusion = bf16[1024,1536]{1,0:T(8,128)(2,1)} fusion(bf16[512,1536]{1,0:T(8,128)(2,1)S(1)} %fusion, s32[1024]{0:T(1024)S(1)} %broadcast_clamp_fusion), kind=kCustom, calls=%fused_computation | custom fusion | bytes 6295552 | tf_op jit(solution)/shard_map/jit(_take)/gather | solution.py:92
  228.6 2.2 select_select_fusion
  230.8 45.7 %all_to_all.5 = bf16[16,1,64,1536]{3,2,1,0:T(8,128)(2,1)S(1)} all-to-all(bf16[16,1,64,1536]{3,2,1,0:T(8,128)(2,1)S(1)} %select_select_fusion), channel_id=1, replica_groups=mesh['gx'=4,'gy'=2,'gz'=16] {'gz'}, dimensions={0} | all-to-all | bytes 6291456 | tf_op jit(solution)/shard_map/all_to_all | solution.py:94
  276.5 1.7 copy.42
  (31 shorter events, 0.9 us)
Async XLA Ops:
  6.5 33.3 %all-gather.3.cloned.1.call-start = ((), (), s32[]{:S(2)}) async-start(), calls=%async_computation.3 | async-start | bytes 4718592 | tf_op jit(solution)/shard_map/all_gather | solution.py:53
  20.9 130.4 %reduce-scatter.3.cloned.1.call-start = ((), (), s32[]{:S(2)}) async-start(), calls=%async_computation.4 | async-start | bytes 11796480 | tf_op jit(solution)/shard_map/reduce_scatter | solution.py:59
  60.1 137.6 %all-gather.5.cloned.1.call-start = ((), (), s32[]{:S(2)}) async-start(), calls=%async_computation.5 | async-start | bytes 3932160 | tf_op jit(solution)/shard_map/all_gather | solution.py:78
  154.8 0.7 copy-start.2
  154.8 0.7 copy-start.3
  158.4 62.9 %reduce-scatter.5.cloned.1.call-start = ((), (), s32[]{:S(2)}) async-start(), calls=%async_computation.6 | async-start | bytes 4718592 | tf_op jit(solution)/shard_map/reduce_scatter | solution.py:81
  206.9 0.7 copy-start.4
  206.9 0.8 copy-start.1
  206.9 14.4 %copy-start = (bf16[2,256,1536]{2,1,0:T(8,128)(2,1)S(1)}, bf16[2,256,1536]{2,1,0:T(8,128)(2,1)}, u32[]{:S(2)}) copy-start(bf16[2,256,1536]{2,1,0:T(8,128)(2,1)} %param.8) | copy-start | bytes 4718596
Sparse Core Ops, SparseCore 0:
  21.1 17.4 all-gather.2
  60.2 91.0 reduce-scatter.2
  158.5 39.1 all-gather.4
  207.1 14.1 reduce-scatter.4
where the time goes:
time: 286 us; the launch traced here: 285 us
  waiting for transfers between devices  143 us (50%)
  blocking collectives  55 us (19%)
  local copies, waits for them, and re-layouts  31.3 us (11%)
  matrix products  31.1 us (11%)
  between operations  13.2 us (5%)
  other arithmetic  10.7 us (4%)
    reduce_scatter x1, waiting for transfers between devices, on_device(): lax.psum_scatter(jnp.dot(rows_all, qkv_mat, preferred_element_type=jnp.fl...  91.2 us
    all_to_all x1, blocking collectives, on_device(): lax.all_to_all(outgoing, 'gz', split_axis=0, concat_axis=0, tiled=True)  45.7 us
    all_gather x1, waiting for transfers between devices, on_device(): head_rows = lax.all_gather(attended, 'gx', axis=0, tiled=True)  39.3 us
    unnamed x12, local copies, waits for them, and re-layouts  21.4 us
    dot_general x1, matrix products, on_device(): jnp.dot(rows_all, qkv_mat, preferred_element_type=jnp.float32)  20.2 us
    reduce_scatter x1, waiting for transfers between devices, on_device(): lax.psum_scatter(jnp.dot(flat_heads, out_mat, preferred_element_type=jnp....  12.6 us
    psum x1, blocking collectives, on_device(): lax.psum((jnp.sum(xf, axis=-1), jnp.sum(xf * xf, axis=-1)), 'gx')  9.3 us
    dot_general x1, matrix products, on_device(): jnp.dot(flat_heads, out_mat, preferred_element_type=jnp.float32)  9.18 us
  transfers between devices with their start and end apart: 4, of which 3 were waited for; matrix products, arithmetic and copies ran while one was open for 7% of the time, Pallas kernels for 0%

commit v1 on v0

v1 whole, which is shorter than its diff:
```python
import functools
import math

import jax
import jax.numpy as jnp
from jax import lax
from jax.experimental import pallas as pl
from jax.experimental.pallas import tpu as pltpu
from jax.sharding import PartitionSpec as P

D = 6144
PATCHES = 256
HALF = PATCHES // 2
BLOCK = 1536
GROUP = 384
CHUNK = 3 * GROUP
RANKS = 16
CAP = 64
IMAGES = 4
EPS = 1e-06
MESH = pl.DeviceIdType.MESH
BF16 = jnp.bfloat16
F32 = jnp.float32

OPP, RIGHT, LEFT, OWN = 0, 1, 2, 3
TWO_RIGHT, TWO_LEFT, RIGHT_HIGH, LEFT_LOW, RIGHT_LOW, LEFT_HIGH = range(6)
LOW = pl.ds(0, HALF)
HIGH = pl.ds(HALF, HALF)


def head_norm(values, gain):
    mean_value = jnp.mean(values, axis=-1, keepdims=True)
    spread = jnp.mean(values * values, axis=-1, keepdims=True) - mean_value * mean_value
    return ((values - mean_value) * lax.rsqrt(spread + EPS) * gain).astype(BF16)


def kernel(
    x_hbm, gain_ref, wq_hbm, q_gain_ref, k_gain_ref, wo_hbm, counts_ref, dest_ref,
    out_hbm,
    x_ref, normed, wq, wo, two, to_right, to_left, from_two_left, from_two_right,
    from_left, from_right, own, attended, partial, other, layer, outgoing, stats, stats_in,
    x_sem, wq_sem, wo_sem, stat_send, stat_recv, norm_send, norm_recv, sum_send, sum_recv,
    att_send, att_recv, part_send, part_recv, route_send, route_recv, local_sem,
):
    gx, gy, gz = lax.axis_index("gx"), lax.axis_index("gy"), lax.axis_index("gz")
    at = {
        OPP: lax.rem(gx + 2, 4),
        RIGHT: lax.rem(gx + 1, 4),
        LEFT: lax.rem(gx + 3, 4),
        OWN: gx,
    }
    line = {role: (at[role], gy, gz) for role in (OPP, RIGHT, LEFT)}
    sibling = (gx, 1 - gy, gz)

    barrier = pltpu.get_barrier_semaphore()
    for role in (OPP, RIGHT, LEFT):
        pl.semaphore_signal(barrier, inc=1, device_id=line[role], device_id_type=MESH)
    pl.semaphore_signal(barrier, inc=1, device_id=sibling, device_id_type=MESH)
    for step in range(1, RANKS):
        pl.semaphore_signal(
            barrier, inc=1, device_id=(gx, gy, lax.rem(gz + step, RANKS)), device_id_type=MESH
        )

    x_copy = pltpu.make_async_copy(x_hbm, x_ref, x_sem)
    x_copy.start()
    wq_copies = {}
    for role in (OPP, RIGHT, LEFT, OWN):
        for k in range(9):
            wq_copies[role, k] = pltpu.make_async_copy(
                wq_hbm.at[at[role] * 3 + k // 3, k % 3],
                wq.at[role, :, pl.ds(k * 128, 128)],
                wq_sem.at[role, k],
            )
            wq_copies[role, k].start()
    wo_copies = []
    for role in (OPP, RIGHT, LEFT, OWN):
        copy = pltpu.make_async_copy(
            wo_hbm.at[pl.ds(pl.multiple_of(at[role] * GROUP, GROUP), GROUP)],
            wo.at[pl.ds(role * GROUP, GROUP)],
            wo_sem.at[role],
        )
        copy.start()
        wo_copies.append(copy)

    x_copy.wait()
    lane = lax.broadcasted_iota(jnp.int32, (PATCHES, 128), 1)
    for image in range(2):
        rows = pl.ds(image * PATCHES, PATCHES)
        xf = x_ref[rows, :].astype(F32)
        both = jnp.where(
            lane == 0,
            jnp.sum(xf, axis=-1, keepdims=True),
            jnp.sum(xf * xf, axis=-1, keepdims=True),
        )
        stats[:, rows] = jnp.transpose(both)[0:8, :]

    pl.semaphore_wait(barrier, 3 + 1 + RANKS - 1)

    mirror = {OPP: OPP, RIGHT: LEFT, LEFT: RIGHT}
    stat_copies = []
    for role in (OPP, RIGHT, LEFT):
        copy = pltpu.make_async_remote_copy(
            src_ref=stats,
            dst_ref=stats_in.at[mirror[role]],
            send_sem=stat_send.at[role],
            recv_sem=stat_recv.at[mirror[role]],
            device_id=line[role],
            device_id_type=MESH,
        )
        copy.start()
        stat_copies.append(copy)
    for copy in stat_copies:
        copy.wait()
    total = stats[...] + stats_in[0] + stats_in[1] + stats_in[2]

    def norm_copy(image):
        return pltpu.make_async_remote_copy(
            src_ref=normed.at[gy * 2 + image],
            dst_ref=normed.at[gy * 2 + image],
            send_sem=norm_send.at[image],
            recv_sem=norm_recv.at[image],
            device_id=sibling,
            device_id_type=MESH,
        )

    for image in range(2):
        rows = pl.ds(image * PATCHES, PATCHES)
        part = total[:, image * PATCHES:(image + 1) * PATCHES]
        column = jnp.transpose(jnp.concatenate([part] * 16, axis=0))
        mean_value = column[:, 0:1] * (1.0 / D)
        spread = column[:, 1:2] * (1.0 / D) - mean_value * mean_value
        scale = lax.rsqrt(spread + EPS)
        xf = x_ref[rows, :].astype(F32)
        normed[gy * 2 + image] = ((xf - mean_value) * scale * gain_ref[...]).astype(BF16)
        norm_copy(image).start()

    def sum_copy(image, kind):
        src, dst, role = {
            TWO_RIGHT: (two.at[image, LOW], from_two_left.at[image], RIGHT),
            TWO_LEFT: (two.at[image, HIGH], from_two_right.at[image], LEFT),
            RIGHT_HIGH: (to_right.at[image, HIGH], from_left.at[image, HIGH], RIGHT),
            LEFT_LOW: (to_left.at[image, LOW], from_right.at[image, LOW], LEFT),
            RIGHT_LOW: (to_right.at[image, LOW], from_left.at[image, LOW], RIGHT),
            LEFT_HIGH: (to_left.at[image, HIGH], from_right.at[image, HIGH], LEFT),
        }[kind]
        return pltpu.make_async_remote_copy(
            src_ref=src,
            dst_ref=dst,
            send_sem=sum_send.at[image, kind],
            recv_sem=sum_recv.at[image, kind],
            device_id=line[role],
            device_id_type=MESH,
        )

    def att_copy(image, role):
        return pltpu.make_async_remote_copy(
            src_ref=attended.at[image, :, pl.ds(OWN * GROUP, GROUP)],
            dst_ref=attended.at[image, :, pl.ds(mirror[role] * GROUP, GROUP)],
            send_sem=att_send.at[image, role],
            recv_sem=att_recv.at[image, mirror[role]],
            device_id=line[role],
            device_id_type=MESH,
        )

    def part_copy(image):
        slot = lax.rem(image, 2)
        return pltpu.make_async_remote_copy(
            src_ref=partial.at[image],
            dst_ref=other.at[slot],
            send_sem=part_send.at[slot],
            recv_sem=part_recv.at[slot],
            device_id=sibling,
            device_id_type=MESH,
        )

    def route_copy(step):
        return pltpu.make_async_remote_copy(
            src_ref=outgoing.at[step],
            dst_ref=out_hbm.at[gz],
            send_sem=route_send.at[step],
            recv_sem=route_recv.at[step],
            device_id=(gx, gy, lax.rem(gz + step, RANKS)),
            device_id_type=MESH,
        )

    def product(image, role):
        return jnp.dot(normed[image], wq[role], preferred_element_type=F32)

    def wait_weights(role):
        for k in range(9):
            wq_copies[role, k].wait()

    def attend(image):
        own[...] = product(image, OWN)
        for kind in (RIGHT_HIGH, LEFT_LOW, RIGHT_LOW, LEFT_HIGH):
            sum_copy(image, kind).wait_recv()
        own[...] += from_left[image].astype(F32) + from_right[image].astype(F32)
        for head in range(3):
            base = head * 384
            query = head_norm(own[:, base:base + 128], q_gain_ref[...])
            keys = head_norm(own[:, base + 128:base + 256], k_gain_ref[...])
            values = own[:, base + 256:base + 384].astype(BF16)
            scores = lax.dot_general(
                query, keys, (((1,), (1,)), ((), ())), preferred_element_type=F32
            ) * (1.0 / math.sqrt(128))
            expo = jnp.exp(scores)
            weights = (expo * (1.0 / jnp.sum(expo, axis=-1, keepdims=True))).astype(BF16)
            attended[image, :, pl.ds(OWN * GROUP + head * 128, 128)] = jnp.dot(
                weights, values, preferred_element_type=F32
            ).astype(BF16)
        for role in (OPP, RIGHT, LEFT):
            att_copy(image, role).start()

    def route():
        for image in range(2):
            part_copy(image).wait_recv()
            rows = pl.ds(image * PATCHES, PATCHES)
            layer[rows, :] = (
                x_ref[rows, :].astype(F32)
                + (partial[gy * 2 + image].astype(F32) + other[image].astype(F32))
            ).astype(BF16)
        row = lax.broadcasted_iota(jnp.int32, (1, 2 * PATCHES), 1)
        target = jnp.full((1, 2 * PATCHES), RANKS * CAP, jnp.int32)
        for image in range(2):
            start = image * PATCHES
            for piece in range(8):
                stop = start + counts_ref[image, piece]
                target = jnp.where(
                    (row >= start) & (row < stop),
                    dest_ref[image, piece] * CAP + row - start,
                    target,
                )
                start = stop
        place = lax.broadcasted_iota(jnp.int32, (4 * CAP, 1), 0)
        for quarter in range(4):
            rank = (gz + 4 * quarter + (place >> 6)) & (RANKS - 1)
            pick = jnp.where((rank * CAP + (place & (CAP - 1))) == target, 1.0, 0.0).astype(BF16)
            picked = jnp.dot(pick, layer[...], preferred_element_type=F32).astype(BF16)
            outgoing[pl.ds(4 * quarter, 4)] = picked.reshape(4, CAP, BLOCK)
            for step in range(4 * quarter, 4 * quarter + 4):
                if step == 0:
                    pltpu.make_async_copy(outgoing.at[0], out_hbm.at[gz], local_sem).start()
                else:
                    route_copy(step).start()

    def turn(step, carry):
        @pl.when((step >= 1) & (step <= IMAGES))
        def _():
            image = lax.rem(step + 3, IMAGES)

            @pl.when(step == 1)
            def _():
                wait_weights(RIGHT)
                wait_weights(LEFT)

            to_right[image] = product(image, RIGHT).astype(BF16)
            sum_copy(image, RIGHT_HIGH).start()
            to_left[image] = product(image, LEFT).astype(BF16)
            sum_copy(image, LEFT_LOW).start()

        @pl.when(step < IMAGES)
        def _():
            image = lax.rem(step, IMAGES)

            @pl.when(image // 2 != gy)
            def _():
                norm_copy(lax.rem(image, 2)).wait_recv()

            @pl.when(step == 0)
            def _():
                wait_weights(OPP)

            two[image] = product(image, OPP).astype(BF16)
            sum_copy(image, TWO_RIGHT).start()
            sum_copy(image, TWO_LEFT).start()

        @pl.when((step >= 1) & (step <= IMAGES))
        def _():
            image = lax.rem(step + 3, IMAGES)
            sum_copy(image, TWO_RIGHT).wait_recv()
            to_right[image, LOW, :] = (
                to_right[image, LOW, :].astype(F32) + from_two_left[image].astype(F32)
            ).astype(BF16)
            sum_copy(image, RIGHT_LOW).start()
            sum_copy(image, TWO_LEFT).wait_recv()
            to_left[image, HIGH, :] = (
                to_left[image, HIGH, :].astype(F32) + from_two_right[image].astype(F32)
            ).astype(BF16)
            sum_copy(image, LEFT_HIGH).start()

        @pl.when((step >= 2) & (step <= IMAGES + 1))
        def _():
            @pl.when(step == 2)
            def _():
                wait_weights(OWN)

            attend(lax.rem(step + 2, IMAGES))

        @pl.when(step >= 3)
        def _():
            image = lax.rem(step + 1, IMAGES)

            @pl.when(step == 3)
            def _():
                for copy in wo_copies:
                    copy.wait()

            for role in (OPP, RIGHT, LEFT):
                att_copy(image, role).wait_recv()
            partial[image] = jnp.dot(
                attended[image], wo[...], preferred_element_type=F32
            ).astype(BF16)

            @pl.when(image // 2 != gy)
            def _():
                part_copy(image).start()

        @pl.when(step == 4 + 2 * gy)
        def _():
            route()

        return carry

    lax.fori_loop(0, IMAGES + 3, turn, 0)

    for image in range(2):
        norm_copy(image).wait_send()
        part_copy(image).wait_send()
    for image in range(IMAGES):
        for kind in range(6):
            sum_copy(image, kind).wait_send()
        for role in (OPP, RIGHT, LEFT):
            att_copy(image, role).wait_send()
    pltpu.make_async_copy(outgoing.at[0], out_hbm.at[gz], local_sem).wait()
    for step in range(1, RANKS):
        route_copy(step).wait()


def on_device(x_in, ln_gain, w_qkv, q_gain, k_gain, w_out, counts, dest):
    any_spec = pl.BlockSpec(memory_space=pl.ANY)
    vmem_spec = pl.BlockSpec(memory_space=pltpu.VMEM)
    smem_spec = pl.BlockSpec(memory_space=pltpu.SMEM)
    dma = pltpu.SemaphoreType.DMA
    routed = pl.pallas_call(
        kernel,
        out_shape=jax.ShapeDtypeStruct((RANKS, CAP, BLOCK), BF16),
        in_specs=[
            any_spec, vmem_spec, any_spec, vmem_spec, vmem_spec, any_spec, smem_spec, smem_spec,
        ],
        out_specs=any_spec,
        scratch_shapes=[
            pltpu.VMEM((2 * PATCHES, BLOCK), BF16),
            pltpu.VMEM((IMAGES, PATCHES, BLOCK), BF16),
            pltpu.VMEM((4, BLOCK, CHUNK), BF16),
            pltpu.VMEM((BLOCK, BLOCK), BF16),
            pltpu.VMEM((IMAGES, PATCHES, CHUNK), BF16),
            pltpu.VMEM((IMAGES, PATCHES, CHUNK), BF16),
            pltpu.VMEM((IMAGES, PATCHES, CHUNK), BF16),
            pltpu.VMEM((IMAGES, HALF, CHUNK), BF16),
            pltpu.VMEM((IMAGES, HALF, CHUNK), BF16),
            pltpu.VMEM((IMAGES, PATCHES, CHUNK), BF16),
            pltpu.VMEM((IMAGES, PATCHES, CHUNK), BF16),
            pltpu.VMEM((PATCHES, CHUNK), F32),
            pltpu.VMEM((IMAGES, PATCHES, BLOCK), BF16),
            pltpu.VMEM((IMAGES, PATCHES, BLOCK), BF16),
            pltpu.VMEM((2, PATCHES, BLOCK), BF16),
            pltpu.VMEM((2 * PATCHES, BLOCK), BF16),
            pltpu.VMEM((RANKS, CAP, BLOCK), BF16),
            pltpu.VMEM((8, 2 * PATCHES), F32),
            pltpu.VMEM((3, 8, 2 * PATCHES), F32),
            dma(()),
            dma((4, 9)),
            dma((4,)),
            dma((3,)),
            dma((3,)),
            dma((2,)),
            dma((2,)),
            dma((IMAGES, 6)),
            dma((IMAGES, 6)),
            dma((IMAGES, 3)),
            dma((IMAGES, 3)),
            dma((2,)),
            dma((2,)),
            dma((RANKS,)),
            dma((RANKS,)),
            dma(()),
        ],
        compiler_params=pltpu.CompilerParams(
            collective_id=0, has_side_effects=True, vmem_limit_bytes=60 * 2**20
        ),
        cost_estimate=pl.CostEstimate(
            flops=20 * 10**9, bytes_accessed=25 * 10**6, transcendentals=10**6
        ),
        name="layer",
    )(
        x_in.reshape(2 * PATCHES, BLOCK),
        ln_gain.reshape(1, BLOCK),
        jnp.transpose(w_qkv, (1, 2, 0, 3)),
        q_gain.reshape(1, 128),
        k_gain.reshape(1, 128),
        w_out.reshape(BLOCK, BLOCK),
        counts,
        dest,
    )
    return routed.reshape(1, 1, RANKS, 1, CAP, BLOCK)


def solution(mesh):
    in_specs = (
        P(("gy", "gz"), None, "gx"),
        P("gx"),
        P("gx", "gy", None, None),
        P(),
        P(),
        P("gy", None, "gx"),
        P(("gy", "gz"), None),
        P(("gy", "gz"), None),
    )
    out_specs = P("gy", "gz", None, None, None, "gx")
    return jax.shard_map(
        on_device, mesh=mesh, in_specs=in_specs, out_specs=out_specs, check_vma=False
    )
```

time: 286 us -> 164 us (0.57)
  Pallas kernels: 0 us -> 159 us
  waiting for transfers between devices: 143 us -> 0 us
  blocking collectives: 55 us -> 0 us
  matrix products: 31.1 us -> 0 us
  local copies, waits for them, and re-layouts: 31.3 us -> 5.13 us
  between operations: 13.2 us -> 0.01 us
  other arithmetic: 10.7 us -> 0 us
    pallas_call x0 -> x1, Pallas kernels: none -> 159 us  [on_device(): pl.pallas_call(kernel, out_shape=jax.ShapeDtypeStruct((RANKS, CAP, BLOCK)...]
    reduce_scatter x2 -> x0, waiting for transfers between devices: 104 us -> none  [the longest x1 91.2 us: on_device(): lax.psum_scatter(jnp.dot(rows_all, qkv_mat, preferred_element_type=jnp.fl...]
    all_to_all x1 -> x0, blocking collectives: 45.7 us -> none  [on_device(): lax.all_to_all(outgoing, 'gz', split_axis=0, concat_axis=0, tiled=True)]
    all_gather x2 -> x0, waiting for transfers between devices: 39.3 us -> none  [the longest x1 39.3 us: on_device(): head_rows = lax.all_gather(attended, 'gx', axis=0, tiled=True)]
    dot_general x4 -> x0, matrix products: 31.1 us -> none  [the longest x1 20.2 us: on_device(): jnp.dot(rows_all, qkv_mat, preferred_element_type=jnp.float32)]
    unnamed x12 -> x1, local copies, waits for them, and re-layouts: 21.4 us -> 3.83 us
    psum x1 -> x0, blocking collectives: 9.3 us -> none  [on_device(): lax.psum((jnp.sum(xf, axis=-1), jnp.sum(xf * xf, axis=-1)), 'gx')]
    gather x1 -> x0, local copies, waits for them, and re-layouts: 5.56 us -> none  [on_device(): jnp.take(layer_out, index.reshape(-1), axis=0)]
  transfers between devices with their start and end apart: 4 -> 0, of which waited for: 3 -> 0; matrix products, arithmetic and copies ran while one was open for 7% -> 0% of each run, Pallas kernels for 0% -> 0%
where the time goes in v1:
time: 164 us
  Pallas kernels  159 us (97%)
  local copies, waits for them, and re-layouts  5.13 us (3%)
    pallas_call x1, Pallas kernels, on_device(): pl.pallas_call(kernel, out_shape=jax.ShapeDtypeStruct((RANKS, CAP, BLOCK)...  159 us
    unnamed x1, local copies, waits for them, and re-layouts  3.83 us

profile of v1, /device:TPU:1, one launch (start us, length us, event | category | flops | bytes accessed | tf_op | source)
XLA Modules:
  0.0 164.0 jit_solution(14528276713524243672)
XLA Ops:
  0.0 1.3 reshape.19.gain_ref
  1.3 158.8 %layer.1 = bf16[16,64,1536]{2,1,0:T(8,128)(2,1)} custom-call(bf16[512,1536]{1,0:T(8,128)(2,1)} %bitcast.11, f32[1,1536]{1,0:T(1,128)} %reshape.19.gain_ref, bf16[12,3,1536,128]{3,2,1,0:T(8,128)(2,1)} %bitcast.9, f32[1,128]{1,0:T(1,128)} %bitcast.12, f32[1,128]{1,0:T(1,128)} %bitcast.13, bf16[1536,1536]{1,0:T(8,128)(2,1)} %bitcast.10, s32[2,8]{1,0:T(2,128)} %counts_ref.1, ...), custom_call_target="tpu_custom_call" | custom-call | flops 20000000000 | bytes 25000000 | tf_op jit(solution)/shard_map/layer/pallas_call | solution.py:344
  160.2 3.8 %copy.11 = bf16[1,1,16,1,64,1536]{5,4,3,2,1,0:T(8,128)(2,1)} copy(bf16[1,1,16,1,64,1536]{5,4,3,2,1,0:T(8,128)(2,1)} %bitcast.8) | data formatting | bytes 6291456

commit v2 on v0

v2 whole, which is shorter than its diff:
```python
import functools
import math

import jax
import jax.numpy as jnp
from jax import lax
from jax.experimental import pallas as pl
from jax.experimental.pallas import tpu as pltpu
from jax.sharding import PartitionSpec as P

D = 6144
PATCHES = 256
HALF = PATCHES // 2
BLOCK = 1536
WIDE = BLOCK // 2
GROUP = 384
SLOTS = 3
RANKS = 16
RING = 4
CAP = 64
IMAGES = 4
UNITS = IMAGES * SLOTS
EPS = 1e-06
MESH = pl.DeviceIdType.MESH
BF16 = jnp.bfloat16
F32 = jnp.float32

OPP, RIGHT, LEFT, OWN = 0, 1, 2, 3
TWO_RIGHT, TWO_LEFT, RIGHT_HIGH, LEFT_LOW, RIGHT_LOW, LEFT_HIGH = range(6)
ATT_RIGHT, ATT_LEFT, PASS_RIGHT, PASS_LEFT = range(4)
LOW = pl.ds(0, HALF)
HIGH = pl.ds(HALF, HALF)


def head_norm(values, gain):
    mean_value = jnp.mean(values, axis=-1, keepdims=True)
    spread = jnp.mean(values * values, axis=-1, keepdims=True) - mean_value * mean_value
    return ((values - mean_value) * lax.rsqrt(spread + EPS) * gain).astype(BF16)


def remote(src, dst, send_sem, recv_sem, device):
    return pltpu.make_async_remote_copy(
        src_ref=src,
        dst_ref=dst,
        send_sem=send_sem,
        recv_sem=recv_sem,
        device_id=device,
        device_id_type=MESH,
    )


def kernel(
    x_hbm, gain_ref, wq_hbm, q_gain_ref, k_gain_ref, wo_hbm, counts_ref, dest_ref,
    out_hbm,
    x_ref, x_half, normed, wq, wo, two, to_right, to_left, from_two_left, from_two_right,
    from_left, from_right, attended, mine, leaving, other, layer, outgoing, middle, target,
    stats, stats_in,
    x_sem, half_sem, wq_sem, wo_sem, half_send, half_recv, target_send, target_recv,
    stat_send, stat_recv, norm_send, norm_recv, sum_send, sum_recv, att_send, att_recv,
    part_send, part_recv, first_send, first_recv, last_send, last_recv, local_sem,
):
    gx, gy, gz = lax.axis_index("gx"), lax.axis_index("gy"), lax.axis_index("gz")
    at = {
        OPP: lax.rem(gx + 2, RING),
        RIGHT: lax.rem(gx + 1, RING),
        LEFT: lax.rem(gx + 3, RING),
        OWN: gx,
    }
    line = {role: (at[role], gy, gz) for role in (OPP, RIGHT, LEFT)}
    sibling = (gx, 1 - gy, gz)
    z_at, y_at = lax.div(gz, RING), lax.rem(gz, RING)
    first_at = (1 - gy) * y_at + gy * z_at
    last_at = (1 - gy) * z_at + gy * y_at

    def plane(first, last):
        return first * (1 + 3 * gy) + last * (4 - 3 * gy)

    barrier = pltpu.get_barrier_semaphore()
    partners = [line[OPP], line[RIGHT], line[LEFT], sibling]
    for step in range(1, RING):
        for core in (gy, 1 - gy):
            partners.append((gx, core, z_at * RING + lax.rem(y_at + step, RING)))
            partners.append((gx, core, lax.rem(z_at + step, RING) * RING + y_at))
    for partner in partners:
        pl.semaphore_signal(barrier, inc=1, device_id=partner, device_id_type=MESH)

    x_copy = pltpu.make_async_copy(x_hbm, x_ref, x_sem)
    x_copy.start()

    def wq_copies(role, slot):
        return [
            pltpu.make_async_copy(
                wq_hbm.at[at[role] * SLOTS + slot, k],
                wq.at[role, slot, :, pl.ds(k * 128, 128)],
                wq_sem.at[role, slot, k],
            )
            for k in range(3)
        ]

    def wo_copies():
        for side in range(2):
            core = gy if side == 1 else 1 - gy
            for slot in range(SLOTS):
                for role in (OPP, RIGHT, LEFT, OWN):
                    row = pl.multiple_of((at[role] * SLOTS + slot) * 128, 128)
                    yield pltpu.make_async_copy(
                        wo_hbm.at[pl.ds(row, 128), pl.ds(pl.multiple_of(core * WIDE, WIDE), WIDE)],
                        wo.at[side, slot, pl.ds(role * 128, 128)],
                        wo_sem.at[side, slot, role],
                    )

    x_copy.wait()
    for slot in range(SLOTS):
        for role in (OPP, RIGHT, LEFT, OWN):
            for copy in wq_copies(role, slot):
                copy.start()
    half_copy = pltpu.make_async_copy(
        x_hbm.at[:, pl.ds(pl.multiple_of(gy * WIDE, WIDE), WIDE)], x_half.at[gy], half_sem
    )
    half_copy.start()
    for copy in wo_copies():
        copy.start()

    lane = lax.broadcasted_iota(jnp.int32, (PATCHES, 128), 1)
    for image in range(2):
        rows = pl.ds(image * PATCHES, PATCHES)
        xf = x_ref[rows, :].astype(F32)
        both = jnp.where(
            lane == 0,
            jnp.sum(xf, axis=-1, keepdims=True),
            jnp.sum(xf * xf, axis=-1, keepdims=True),
        )
        stats[:, rows] = jnp.transpose(both)[0:8, :]

    pl.semaphore_wait(barrier, len(partners))

    mirror = {OPP: OPP, RIGHT: LEFT, LEFT: RIGHT}
    stat_copies = [
        remote(
            stats, stats_in.at[mirror[role]], stat_send.at[role], stat_recv.at[mirror[role]],
            line[role],
        )
        for role in (OPP, RIGHT, LEFT)
    ]
    for copy in stat_copies:
        copy.start()

    row = lax.broadcasted_iota(jnp.int32, (8, 2 * PATCHES), 1)
    places = jnp.full((8, 2 * PATCHES), RANKS * CAP, jnp.int32)
    for image in range(2):
        begin = image * PATCHES
        for piece in range(8):
            stop = begin + counts_ref[image, piece]
            places = jnp.where(
                (row >= begin) & (row < stop), dest_ref[image, piece] * CAP + row - begin, places
            )
            begin = stop
    target[gy] = places

    for copy in stat_copies:
        copy.wait()
    total = stats[...] + stats_in[0] + stats_in[1] + stats_in[2]

    def norm_copy(image):
        held = normed.at[gy * 2 + image]
        return remote(held, held, norm_send.at[image], norm_recv.at[image], sibling)

    for image in range(2):
        rows = pl.ds(image * PATCHES, PATCHES)
        part = total[:, image * PATCHES:(image + 1) * PATCHES]
        column = jnp.transpose(jnp.concatenate([part] * 16, axis=0))
        mean_value = column[:, 0:1] * (1.0 / D)
        spread = column[:, 1:2] * (1.0 / D) - mean_value * mean_value
        scale = lax.rsqrt(spread + EPS)
        xf = x_ref[rows, :].astype(F32)
        normed[gy * 2 + image] = ((xf - mean_value) * scale * gain_ref[...].reshape(1, BLOCK)).astype(BF16)
        norm_copy(image).start()

    target_copy = remote(target.at[gy], target.at[gy], target_send, target_recv, sibling)
    target_copy.start()
    cross_copy = remote(
        x_hbm.at[:, pl.ds(pl.multiple_of((1 - gy) * WIDE, WIDE), WIDE)],
        x_half.at[gy], half_send, half_recv, sibling,
    )
    cross_copy.start()

    def sum_copy(unit, kind):
        src, dst, role = {
            TWO_RIGHT: (two.at[unit, LOW], from_two_left.at[unit], RIGHT),
            TWO_LEFT: (two.at[unit, HIGH], from_two_right.at[unit], LEFT),
            RIGHT_HIGH: (to_right.at[unit, HIGH], from_left.at[unit, HIGH], RIGHT),
            LEFT_LOW: (to_left.at[unit, LOW], from_right.at[unit, LOW], LEFT),
            RIGHT_LOW: (to_right.at[unit, LOW], from_left.at[unit, LOW], RIGHT),
            LEFT_HIGH: (to_left.at[unit, HIGH], from_right.at[unit, HIGH], LEFT),
        }[kind]
        return remote(src, dst, sum_send.at[unit, kind], sum_recv.at[unit, kind], line[role])

    def att_copy(unit, kind):
        every = pl.ds(0, PATCHES)
        rows, source, place, role = {
            ATT_RIGHT: (every, OWN, LEFT, RIGHT),
            ATT_LEFT: (every, OWN, RIGHT, LEFT),
            PASS_RIGHT: (LOW, LEFT, OPP, RIGHT),
            PASS_LEFT: (HIGH, RIGHT, OPP, LEFT),
        }[kind]
        return remote(
            attended.at[unit, rows, pl.ds(source * 128, 128)],
            attended.at[unit, rows, pl.ds(place * 128, 128)],
            att_send.at[unit, kind], att_recv.at[unit, kind], line[role],
        )

    def part_copy(image):
        return remote(
            leaving.at[image], other.at[image], part_send.at[image], part_recv.at[image], sibling
        )

    def first_copy(group, step):
        return remote(
            outgoing.at[group, step - 1], middle.at[group, :, first_at],
            first_send.at[group, step - 1], first_recv.at[group, step - 1],
            (gx, gy, plane(lax.rem(first_at + step, RING), last_at)),
        )

    columns = {core: pl.ds(core * WIDE, WIDE) for core in range(2)}

    def last_copy(group, step, core):
        to = lax.rem(last_at + step, RING)
        if core == 0:
            dst = out_hbm.at[last_at, :, :, columns[core]]
        else:
            dst = out_hbm.at[:, last_at, :, columns[core]]
        return remote(
            middle.at[group, to], dst, last_send.at[group, step], last_recv.at[core, step],
            (gx, group, plane(first_at, to)),
        )

    def stay_copy(group, core):
        if core == 0:
            dst = out_hbm.at[last_at, :, :, columns[core]]
        else:
            dst = out_hbm.at[:, last_at, :, columns[core]]
        return pltpu.make_async_copy(middle.at[group, last_at], dst, local_sem)

    def product(unit, role):
        return jnp.dot(
            normed[lax.div(unit, SLOTS)], wq[role, lax.rem(unit, SLOTS)],
            preferred_element_type=F32,
        )

    def wait_weights(role, unit):
        for copy in wq_copies(role, lax.rem(unit, SLOTS)):
            copy.wait()

    def attend(unit):
        own = product(unit, OWN)
        for kind in (RIGHT_HIGH, LEFT_LOW, RIGHT_LOW, LEFT_HIGH):
            sum_copy(unit, kind).wait_recv()
        qkv = own + (from_left[unit].astype(F32) + from_right[unit].astype(F32))
        query = head_norm(qkv[:, 0:128], q_gain_ref[...])
        keys = head_norm(qkv[:, 128:256], k_gain_ref[...])
        values = qkv[:, 256:384].astype(BF16)
        scores = lax.dot_general(
            query, keys, (((1,), (1,)), ((), ())), preferred_element_type=F32
        ) * (1.0 / math.sqrt(128))
        expo = jnp.exp(scores)
        weights = (expo * (1.0 / jnp.sum(expo, axis=-1, keepdims=True))).astype(BF16)
        attended[unit, :, pl.ds(OWN * 128, 128)] = jnp.dot(
            weights, values, preferred_element_type=F32
        ).astype(BF16)
        att_copy(unit, ATT_RIGHT).start()
        att_copy(unit, ATT_LEFT).start()

    def project(image, side):
        parts = [
            jnp.dot(attended[image * SLOTS + slot], wo[side, slot], preferred_element_type=F32)
            for slot in range(SLOTS)
        ]
        return (parts[0] + parts[1] + parts[2]).astype(BF16)

    def route(group):
        for image in range(2):
            held = group * 2 + image
            part_copy(held).wait_recv()
            rows = pl.ds(image * PATCHES, PATCHES)
            layer[rows, :] = (
                x_half[group, rows, :].astype(F32)
                + (mine[held].astype(F32) + other[held].astype(F32))
            ).astype(BF16)
        place = lax.broadcasted_iota(jnp.int32, (RING * CAP, 1), 0)
        places = target[group][0:1, :]
        for step in (2, 1, 3, 0):
            rank = plane(lax.rem(first_at + step, RING), place >> 6)
            pick = jnp.where(rank * CAP + (place & (CAP - 1)) == places, 1.0, 0.0).astype(BF16)
            picked = jnp.dot(pick, layer[...], preferred_element_type=F32).astype(BF16)
            picked = picked.reshape(RING, CAP, WIDE)
            if step == 0:
                for to in range(RING):
                    middle[group, to, first_at] = picked[to]
            else:
                outgoing[group, step - 1] = picked
                first_copy(group, step).start()

    def route_on(group):
        for step in range(1, RING):
            first_copy(group, step).wait_recv()
        for core in range(2):
            @pl.when(gy == core)
            def _():
                for step in (2, 1, 3):
                    last_copy(group, step, core).start()

                @pl.when(group == gy)
                def _():
                    stay_copy(group, core).start()

                @pl.when(group != gy)
                def _():
                    last_copy(group, 0, core).start()

    def turn(step, carry):
        def back(count):
            return lax.rem(step + UNITS - count, UNITS)

        @pl.when((step >= 1) & (step <= UNITS))
        def _():
            unit = back(1)

            @pl.when(step <= SLOTS)
            def _():
                wait_weights(RIGHT, unit)
                wait_weights(LEFT, unit)

            to_right[unit] = product(unit, RIGHT).astype(BF16)
            sum_copy(unit, RIGHT_HIGH).start()
            to_left[unit] = product(unit, LEFT).astype(BF16)
            sum_copy(unit, LEFT_LOW).start()

        @pl.when(step < UNITS)
        def _():
            unit = back(0)
            image = lax.div(unit, SLOTS)

            @pl.when((lax.rem(unit, SLOTS) == 0) & (lax.div(image, 2) != gy))
            def _():
                norm_copy(lax.rem(image, 2)).wait_recv()

            @pl.when(step < SLOTS)
            def _():
                wait_weights(OPP, unit)

            two[unit] = product(unit, OPP).astype(BF16)
            sum_copy(unit, TWO_RIGHT).start()
            sum_copy(unit, TWO_LEFT).start()

        @pl.when((step >= 1) & (step <= UNITS))
        def _():
            unit = back(1)
            sum_copy(unit, TWO_RIGHT).wait_recv()
            to_right[unit, LOW, :] = (
                to_right[unit, LOW, :].astype(F32) + from_two_left[unit].astype(F32)
            ).astype(BF16)
            sum_copy(unit, RIGHT_LOW).start()
            sum_copy(unit, TWO_LEFT).wait_recv()
            to_left[unit, HIGH, :] = (
                to_left[unit, HIGH, :].astype(F32) + from_two_right[unit].astype(F32)
            ).astype(BF16)
            sum_copy(unit, LEFT_HIGH).start()

        @pl.when((step >= 2) & (step <= UNITS + 1))
        def _():
            unit = back(2)

            @pl.when(step < SLOTS + 2)
            def _():
                wait_weights(OWN, unit)

            attend(unit)

        @pl.when((step >= 3) & (step <= UNITS + 2))
        def _():
            unit = back(3)
            att_copy(unit, ATT_RIGHT).wait_recv()
            att_copy(unit, PASS_RIGHT).start()
            att_copy(unit, ATT_LEFT).wait_recv()
            att_copy(unit, PASS_LEFT).start()

        @pl.when((step >= 6) & (lax.rem(step, SLOTS) == 0))
        def _():
            image = lax.rem(lax.div(step, SLOTS) + 2, IMAGES)

            @pl.when(step == 6)
            def _():
                for copy in wo_copies():
                    copy.wait()
                half_copy.wait()
                target_copy.wait()
                cross_copy.wait()

            for slot in range(SLOTS):
                att_copy(image * SLOTS + slot, PASS_RIGHT).wait_recv()
                att_copy(image * SLOTS + slot, PASS_LEFT).wait_recv()
            leaving[image] = project(image, 0)
            part_copy(image).start()
            mine[image] = project(image, 1)

        @pl.when((step == 10) | (step == 15))
        def _():
            route(lax.div(step, 15))

        @pl.when((step == 12) | (step == 16))
        def _():
            route_on(lax.div(step, 16))

        return carry

    lax.fori_loop(0, UNITS + 5, turn, 0)

    def drain(unit, carry):
        for kind in range(6):
            sum_copy(unit, kind).wait_send()
        for kind in range(4):
            att_copy(unit, kind).wait_send()
        return carry

    lax.fori_loop(0, UNITS, drain, 0)
    for image in range(2):
        norm_copy(image).wait_send()
    for image in range(IMAGES):
        part_copy(image).wait_send()
    for group in range(2):
        for step in range(1, RING):
            first_copy(group, step).wait_send()
            last_copy(group, step, group).wait_send()
            last_copy(group, step, group).wait_recv()

        @pl.when(group != gy)
        def _():
            last_copy(group, 0, 0).wait_send()

    for core in range(2):
        @pl.when(core != gy)
        def _():
            last_copy(core, 0, core).wait_recv()

        @pl.when(core == gy)
        def _():
            stay_copy(core, core).wait()


def on_device(x_in, ln_gain, w_qkv, q_gain, k_gain, w_out, counts, dest):
    any_spec = pl.BlockSpec(memory_space=pl.ANY)
    vmem_spec = pl.BlockSpec(memory_space=pltpu.VMEM)
    smem_spec = pl.BlockSpec(memory_space=pltpu.SMEM)
    dma = pltpu.SemaphoreType.DMA
    routed = pl.pallas_call(
        kernel,
        out_shape=pltpu.VMEM((RING, RING, CAP, BLOCK), BF16),
        in_specs=[
            any_spec, vmem_spec, any_spec, vmem_spec, vmem_spec, any_spec, smem_spec, smem_spec,
        ],
        out_specs=any_spec,
        scratch_shapes=[
            pltpu.VMEM((2 * PATCHES, BLOCK), BF16),
            pltpu.VMEM((2, 2 * PATCHES, WIDE), BF16),
            pltpu.VMEM((IMAGES, PATCHES, BLOCK), BF16),
            pltpu.VMEM((4, SLOTS, BLOCK, GROUP), BF16),
            pltpu.VMEM((2, SLOTS, 4 * 128, WIDE), BF16),
            pltpu.VMEM((UNITS, PATCHES, GROUP), BF16),
            pltpu.VMEM((UNITS, PATCHES, GROUP), BF16),
            pltpu.VMEM((UNITS, PATCHES, GROUP), BF16),
            pltpu.VMEM((UNITS, HALF, GROUP), BF16),
            pltpu.VMEM((UNITS, HALF, GROUP), BF16),
            pltpu.VMEM((UNITS, PATCHES, GROUP), BF16),
            pltpu.VMEM((UNITS, PATCHES, GROUP), BF16),
            pltpu.VMEM((UNITS, PATCHES, 4 * 128), BF16),
            pltpu.VMEM((IMAGES, PATCHES, WIDE), BF16),
            pltpu.VMEM((IMAGES, PATCHES, WIDE), BF16),
            pltpu.VMEM((IMAGES, PATCHES, WIDE), BF16),
            pltpu.VMEM((2 * PATCHES, WIDE), BF16),
            pltpu.VMEM((2, RING - 1, RING, CAP, WIDE), BF16),
            pltpu.VMEM((2, RING, RING, CAP, WIDE), BF16),
            pltpu.VMEM((2, 8, 2 * PATCHES), jnp.int32),
            pltpu.VMEM((8, 2 * PATCHES), F32),
            pltpu.VMEM((3, 8, 2 * PATCHES), F32),
            dma(()),
            dma(()),
            dma((4, SLOTS, 3)),
            dma((2, SLOTS, 4)),
            dma(()),
            dma(()),
            dma(()),
            dma(()),
            dma((3,)),
            dma((3,)),
            dma((2,)),
            dma((2,)),
            dma((UNITS, 6)),
            dma((UNITS, 6)),
            dma((UNITS, 4)),
            dma((UNITS, 4)),
            dma((IMAGES,)),
            dma((IMAGES,)),
            dma((2, RING - 1)),
            dma((2, RING - 1)),
            dma((2, RING)),
            dma((2, RING)),
            dma(()),
        ],
        compiler_params=pltpu.CompilerParams(
            collective_id=0, has_side_effects=True, vmem_limit_bytes=58 * 2**20
        ),
        cost_estimate=pl.CostEstimate(
            flops=20 * 10**9, bytes_accessed=25 * 10**6, transcendentals=10**6
        ),
        name="layer",
    )(
        x_in.reshape(2 * PATCHES, BLOCK),
        ln_gain,
        jnp.transpose(w_qkv, (1, 2, 0, 3)),
        q_gain.reshape(1, 128),
        k_gain.reshape(1, 128),
        w_out.reshape(BLOCK, BLOCK),
        counts,
        dest,
    )
    return routed.reshape(1, 1, RANKS, 1, CAP, BLOCK)


def solution(mesh):
    in_specs = (
        P(("gy", "gz"), None, "gx"),
        P("gx"),
        P("gx", "gy", None, None),
        P(),
        P(),
        P("gy", None, "gx"),
        P(("gy", "gz"), None),
        P(("gy", "gz"), None),
    )
    out_specs = P("gy", "gz", None, None, None, "gx")
    return jax.shard_map(
        on_device, mesh=mesh, in_specs=in_specs, out_specs=out_specs, check_vma=False
    )
```

time: 286 us -> 151 us (0.53)
  Pallas kernels: 0 us -> 149 us
  waiting for transfers between devices: 143 us -> 0 us
  blocking collectives: 55 us -> 0 us
  matrix products: 31.1 us -> 0 us
  local copies, waits for them, and re-layouts: 31.3 us -> 1.67 us
  between operations: 13.2 us -> 0.01 us
  other arithmetic: 10.7 us -> 0 us
    pallas_call x0 -> x1, Pallas kernels: none -> 149 us  [on_device(): pl.pallas_call(kernel, out_shape=pltpu.VMEM((RING, RING, CAP, BLOCK), BF1...]
    reduce_scatter x2 -> x0, waiting for transfers between devices: 104 us -> none  [the longest x1 91.2 us: on_device(): lax.psum_scatter(jnp.dot(rows_all, qkv_mat, preferred_element_type=jnp.fl...]
    all_to_all x1 -> x0, blocking collectives: 45.7 us -> none  [on_device(): lax.all_to_all(outgoing, 'gz', split_axis=0, concat_axis=0, tiled=True)]
    all_gather x2 -> x0, waiting for transfers between devices: 39.3 us -> none  [the longest x1 39.3 us: on_device(): head_rows = lax.all_gather(attended, 'gx', axis=0, tiled=True)]
    dot_general x4 -> x0, matrix products: 31.1 us -> none  [the longest x1 20.2 us: on_device(): jnp.dot(rows_all, qkv_mat, preferred_element_type=jnp.float32)]
    unnamed x12 -> x1, local copies, waits for them, and re-layouts: 21.4 us -> 1.67 us
    psum x1 -> x0, blocking collectives: 9.3 us -> none  [on_device(): lax.psum((jnp.sum(xf, axis=-1), jnp.sum(xf * xf, axis=-1)), 'gx')]
    gather x1 -> x0, local copies, waits for them, and re-layouts: 5.56 us -> none  [on_device(): jnp.take(layer_out, index.reshape(-1), axis=0)]
  transfers between devices with their start and end apart: 4 -> 0, of which waited for: 3 -> 0; matrix products, arithmetic and copies ran while one was open for 7% -> 0% of each run, Pallas kernels for 0% -> 0%
where the time goes in v2:
time: 151 us
  Pallas kernels  149 us (99%)
  local copies, waits for them, and re-layouts  1.67 us (1%)
    pallas_call x1, Pallas kernels, on_device(): pl.pallas_call(kernel, out_shape=pltpu.VMEM((RING, RING, CAP, BLOCK), BF1...  149 us

profile of v2, /device:TPU:1, one launch (start us, length us, event | category | flops | bytes accessed | tf_op | source)
XLA Modules:
  0.0 151.0 jit_solution(4710443810061558723)
XLA Ops:
  0.0 149.3 %layer.1 = bf16[4,4,64,1536]{3,2,1,0:T(8,128)(2,1)S(1)} custom-call(bf16[512,1536]{1,0:T(8,128)(2,1)} %bitcast.11, f32[1536]{0:T(1024)} %gain_ref.1, bf16[12,3,1536,128]{3,2,1,0:T(8,128)(2,1)} %bitcast.9, f32[1,128]{1,0:T(1,128)} %bitcast.12, f32[1,128]{1,0:T(1,128)} %bitcast.13, bf16[1536,1536]{1,0:T(8,128)(2,1)} %bitcast.10, s32[2,8]{1,0:T(2,128)} %counts_ref.1, ...), custom_call_target="tpu_custom_call" | custom-call | flops 20000000000 | bytes 25000000 | tf_op jit(solution)/shard_map/layer/pallas_call | solution.py:455
  149.3 1.7 %copy.11 = bf16[1,1,16,1,64,1536]{5,4,3,2,1,0:T(8,128)(2,1)} copy(bf16[1,1,16,1,64,1536]{5,4,3,2,1,0:T(8,128)(2,1)S(1)} %bitcast.8) | data formatting | bytes 6291456

commit v3 on v2

v3 whole, which is shorter than its diff:
```python
import functools
import math

import jax
import jax.numpy as jnp
from jax import lax
from jax.experimental import pallas as pl
from jax.experimental.pallas import tpu as pltpu
from jax.sharding import PartitionSpec as P

D = 6144
PATCHES = 256
HALF = PATCHES // 2
BLOCK = 1536
WIDE = BLOCK // 2
GROUP = 384
SLOTS = 3
RANKS = 16
RING = 4
CAP = 64
IMAGES = 4
UNITS = IMAGES * SLOTS
EPS = 1e-06
MESH = pl.DeviceIdType.MESH
BF16 = jnp.bfloat16
F32 = jnp.float32

OPP, RIGHT, LEFT, OWN = 0, 1, 2, 3
TWO_RIGHT, TWO_LEFT, RIGHT_HIGH, LEFT_LOW, RIGHT_LOW, LEFT_HIGH = range(6)
ATT_RIGHT, ATT_LEFT, PASS_RIGHT, PASS_LEFT = range(4)
LOW = pl.ds(0, HALF)
HIGH = pl.ds(HALF, HALF)


def head_norm(values, gain):
    mean_value = jnp.mean(values, axis=-1, keepdims=True)
    spread = jnp.mean(values * values, axis=-1, keepdims=True) - mean_value * mean_value
    return ((values - mean_value) * lax.rsqrt(spread + EPS) * gain).astype(BF16)


def remote(src, dst, send_sem, recv_sem, device):
    return pltpu.make_async_remote_copy(
        src_ref=src,
        dst_ref=dst,
        send_sem=send_sem,
        recv_sem=recv_sem,
        device_id=device,
        device_id_type=MESH,
    )


def kernel(
    x_hbm, gain_hbm, wq_hbm, q_gain_hbm, k_gain_hbm, wo_hbm, counts_hbm, dest_hbm,
    out_hbm,
    x_ref, gain_ref, q_gain_ref, k_gain_ref, counts_ref, dest_ref, x_half, normed, wq, wo, two, to_right, to_left, from_two_left, from_two_right,
    from_left, from_right, attended, held, lead, fix, lead_out, lead_in, mine, leaving, other, layer, picks, outgoing, middle, target,
    stats, stats_in,
    x_sem, small_sem, half_sem, wq_sem, wo_sem, half_send, half_recv, target_send, target_recv,
    stat_send, stat_recv, lead_send, lead_recv, norm_send, norm_recv, sum_send, sum_recv, att_send, att_recv,
    part_send, part_recv, first_send, first_recv, last_send, last_recv, local_sem,
):
    gx, gy, gz = lax.axis_index("gx"), lax.axis_index("gy"), lax.axis_index("gz")
    at = {
        OPP: lax.rem(gx + 2, RING),
        RIGHT: lax.rem(gx + 1, RING),
        LEFT: lax.rem(gx + 3, RING),
        OWN: gx,
    }
    line = {role: (at[role], gy, gz) for role in (OPP, RIGHT, LEFT)}
    sibling = (gx, 1 - gy, gz)
    z_at, y_at = lax.div(gz, RING), lax.rem(gz, RING)
    first_at = (1 - gy) * y_at + gy * z_at
    last_at = (1 - gy) * z_at + gy * y_at

    def plane(first, last):
        return first * (1 + 3 * gy) + last * (4 - 3 * gy)

    def on_first(step):
        return plane(lax.rem(first_at + step, RING), last_at)

    def on_last(step):
        return plane(first_at, lax.rem(last_at + step, RING))

    barrier = pltpu.get_barrier_semaphore()
    partners = [line[OPP], line[RIGHT], line[LEFT], sibling]
    for step in range(1, RING):
        partners.append((gx, gy, on_first(step)))
        partners.append((gx, gy, on_last(step)))
        partners.append((gx, 1 - gy, on_first(step)))
    for partner in partners:
        pl.semaphore_signal(barrier, inc=1, device_id=partner, device_id_type=MESH)

    rows_of = [pl.ds(image * PATCHES, PATCHES) for image in range(2)]
    x_copies = [
        pltpu.make_async_copy(x_hbm.at[rows], x_ref.at[rows], x_sem.at[image])
        for image, rows in enumerate(rows_of)
    ]
    x_copies[0].start()
    small_copies = [
        pltpu.make_async_copy(src, dst, small_sem.at[k])
        for k, (src, dst) in enumerate((
            (gain_hbm, gain_ref), (q_gain_hbm, q_gain_ref), (k_gain_hbm, k_gain_ref),
            (counts_hbm, counts_ref), (dest_hbm, dest_ref),
        ))
    ]
    for copy in small_copies:
        copy.start()
    x_copies[1].start()

    def wq_copies(role, slot):
        return [
            pltpu.make_async_copy(
                wq_hbm.at[at[role] * SLOTS + slot, k],
                wq.at[role, slot, :, pl.ds(k * 128, 128)],
                wq_sem.at[role, slot, k],
            )
            for k in range(3)
        ]

    def wo_copies():
        for side in range(2):
            core = gy if side == 1 else 1 - gy
            for slot in range(SLOTS):
                for role in (OPP, RIGHT, LEFT, OWN):
                    row = pl.multiple_of((at[role] * SLOTS + slot) * 128, 128)
                    yield pltpu.make_async_copy(
                        wo_hbm.at[pl.ds(row, 128), pl.ds(pl.multiple_of(core * WIDE, WIDE), WIDE)],
                        wo.at[side, slot, pl.ds(role * 128, 128)],
                        wo_sem.at[side, slot, role],
                    )

    half_copy = pltpu.make_async_copy(
        x_hbm.at[:, pl.ds(pl.multiple_of(gy * WIDE, WIDE), WIDE)], x_half.at[gy], half_sem
    )

    def wait_weights(role, slot):
        for copy in wq_copies(role, slot):
            copy.wait()

    for role in (OPP, RIGHT, LEFT):
        for copy in wq_copies(role, 0):
            copy.start()
    def sum_copy(unit, kind):
        src, dst, role = {
            TWO_RIGHT: (two.at[unit, LOW], from_two_left.at[unit], RIGHT),
            TWO_LEFT: (two.at[unit, HIGH], from_two_right.at[unit], LEFT),
            RIGHT_HIGH: (to_right.at[unit, HIGH], from_left.at[unit, HIGH], RIGHT),
            LEFT_LOW: (to_left.at[unit, LOW], from_right.at[unit, LOW], LEFT),
            RIGHT_LOW: (to_right.at[unit, LOW], from_left.at[unit, LOW], RIGHT),
            LEFT_HIGH: (to_left.at[unit, HIGH], from_right.at[unit, HIGH], LEFT),
        }[kind]
        return remote(src, dst, sum_send.at[unit, kind], sum_recv.at[unit, kind], line[role])

    lane = lax.broadcasted_iota(jnp.int32, (PATCHES, 128), 1)
    mirror = {OPP: OPP, RIGHT: LEFT, LEFT: RIGHT}

    def stat_copies(image):
        return [
            remote(
                stats.at[image], stats_in.at[image, mirror[role]], stat_send.at[image, role],
                stat_recv.at[image, mirror[role]], line[role],
            )
            for role in (OPP, RIGHT, LEFT)
        ]

    def add_up(image):
        x_copies[image].wait()
        xf = x_ref[rows_of[image], :].astype(F32)
        sums = jnp.sum(xf, axis=-1, keepdims=True)
        both = jnp.where(lane == 0, sums, jnp.sum(xf * xf, axis=-1, keepdims=True))
        stats[image] = jnp.transpose(both)[0:8, :]
        return xf, sums

    for copy in small_copies:
        copy.wait()
    gain = gain_ref[...].reshape(1, BLOCK)
    xf, sums = add_up(0)
    lead[pl.ds(0, PATCHES), :] = ((xf - sums * (1.0 / BLOCK)) * gain).astype(BF16)
    high = gain.astype(BF16).astype(F32)
    line_at = lax.broadcasted_iota(jnp.int32, (16, BLOCK), 0)
    lead[pl.ds(PATCHES, 16), :] = jnp.where(
        line_at == 0, high, jnp.where(line_at == 1, gain - high, 0.0)
    ).astype(BF16)

    first_unit = 2 * SLOTS * gy

    def lead_product(role):
        full = jnp.dot(lead[...], wq[role, 0], preferred_element_type=F32)
        lead_out[role] = jnp.broadcast_to(
            full[PATCHES:PATCHES + 1, :] + full[PATCHES + 1:PATCHES + 2, :], (8, GROUP)
        )
        return full[0:PATCHES, :]

    lead_copies = [
        remote(
            lead_out.at[role], lead_in.at[mirror[role]], lead_send.at[role],
            lead_recv.at[mirror[role]], line[role],
        )
        for role in (OPP, RIGHT, LEFT)
    ]

    wait_weights(OPP, 0)
    two[first_unit] = lead_product(OPP).astype(BF16)
    for slot in range(SLOTS):
        for role in (OPP, RIGHT, LEFT, OWN):
            if slot != 0 or role == OWN:
                for copy in wq_copies(role, slot):
                    copy.start()

    pl.semaphore_wait(barrier, len(partners))

    for copy in stat_copies(0):
        copy.start()
    sum_copy(first_unit, TWO_RIGHT).start()
    sum_copy(first_unit, TWO_LEFT).start()
    wait_weights(RIGHT, 0)
    to_right[first_unit] = lead_product(RIGHT).astype(BF16)
    sum_copy(first_unit, RIGHT_HIGH).start()
    wait_weights(LEFT, 0)
    to_left[first_unit] = lead_product(LEFT).astype(BF16)
    sum_copy(first_unit, LEFT_LOW).start()
    add_up(1)
    for copy in stat_copies(1):
        copy.start()
    for copy in lead_copies:
        copy.start()

    def norm_copy(image):
        moved = normed.at[gy * 2 + image]
        return remote(moved, moved, norm_send.at[image], norm_recv.at[image], sibling)

    def normalize(image):
        for copy in stat_copies(image):
            copy.wait()
        shares = [stats_in[image, OPP], stats_in[image, RIGHT], stats_in[image, LEFT], stats[image]]
        total = shares[0] + shares[1] + shares[2] + shares[3]
        line_at = lax.broadcasted_iota(jnp.int32, (8, PATCHES), 0)
        part = jnp.where(line_at == 5, total[1:2, :], 0.0)
        for k, share in enumerate(shares + [total]):
            part = jnp.where(line_at == k, share[0:1, :], part)
        column = jnp.transpose(jnp.concatenate([part] * 16, axis=0))
        mean_value = column[:, 4:5] * (1.0 / D)
        spread = column[:, 5:6] * (1.0 / D) - mean_value * mean_value
        scale = lax.rsqrt(spread + EPS)
        if image == 0:
            fix[...] = jnp.where(lane == 4, scale, column * (1.0 / BLOCK) - mean_value)
        xf = x_ref[rows_of[image], :].astype(F32)
        normed[gy * 2 + image] = (
            (xf - mean_value) * scale * gain_ref[...].reshape(1, BLOCK)
        ).astype(BF16)
        norm_copy(image).start()

    def att_copy(unit, kind):
        every = pl.ds(0, PATCHES)
        rows, source, place, role = {
            ATT_RIGHT: (every, OWN, LEFT, RIGHT),
            ATT_LEFT: (every, OWN, RIGHT, LEFT),
            PASS_RIGHT: (LOW, LEFT, OPP, RIGHT),
            PASS_LEFT: (HIGH, RIGHT, OPP, LEFT),
        }[kind]
        return remote(
            attended.at[unit, rows, pl.ds(source * 128, 128)],
            attended.at[unit, rows, pl.ds(place * 128, 128)],
            att_send.at[unit, kind], att_recv.at[unit, kind], line[role],
        )

    def part_copy(image):
        return remote(
            leaving.at[image], other.at[image], part_send.at[image], part_recv.at[image], sibling
        )

    def first_copy(group, step):
        return remote(
            outgoing.at[group, step - 1], middle.at[group, :, first_at],
            first_send.at[group, step - 1], first_recv.at[group, step - 1],
            (gx, gy, on_first(step)),
        )

    columns = {core: pl.ds(core * WIDE, WIDE) for core in range(2)}

    def landing(core, source):
        if core == 0:
            return out_hbm.at[last_at, source, :, columns[core]]
        return out_hbm.at[source, last_at, :, columns[core]]

    def last_copy(group, hop, step, core):
        source = lax.rem(first_at + RING - hop, RING)
        return remote(
            middle.at[group, lax.rem(last_at + step, RING), source], landing(core, source),
            last_send.at[group, hop, step], last_recv.at[core, hop, step],
            (gx, group, on_last(step)),
        )

    def stay_copy(group, hop, core):
        source = lax.rem(first_at + RING - hop, RING)
        return pltpu.make_async_copy(
            middle.at[group, last_at, source], landing(core, source), local_sem.at[hop]
        )

    def product(unit, role):
        return jnp.dot(
            normed[lax.div(unit, SLOTS)], wq[role, lax.rem(unit, SLOTS)],
            preferred_element_type=F32,
        )

    def mend(values):
        for role in (OPP, RIGHT, LEFT):
            values = values + fix[:, role:role + 1] * lead_in[role][0:1, :]
        return fix[:, 4:5] * (values + fix[:, OWN:OWN + 1] * lead_out[OWN][0:1, :])

    def attend(unit, is_first):
        @pl.when(is_first)
        def _():
            held[...] = lead_product(OWN)
            for copy in lead_copies:
                copy.wait_recv()

        @pl.when(jnp.logical_not(is_first))
        def _():
            held[...] = product(unit, OWN)

        for kind in (RIGHT_HIGH, LEFT_LOW, RIGHT_LOW, LEFT_HIGH):
            sum_copy(unit, kind).wait_recv()
        held[...] += from_left[unit].astype(F32) + from_right[unit].astype(F32)

        @pl.when(is_first)
        def _():
            held[...] = mend(held[...])

        qkv = held[...]
        query = head_norm(qkv[:, 0:128], q_gain_ref[...])
        keys = head_norm(qkv[:, 128:256], k_gain_ref[...])
        values = qkv[:, 256:384].astype(BF16)
        scores = lax.dot_general(
            query, keys, (((1,), (1,)), ((), ())), preferred_element_type=F32
        ) * (1.0 / math.sqrt(128))
        expo = jnp.exp(scores)
        weights = (expo * (1.0 / jnp.sum(expo, axis=-1, keepdims=True))).astype(BF16)
        attended[unit, :, pl.ds(OWN * 128, 128)] = jnp.dot(
            weights, values, preferred_element_type=F32
        ).astype(BF16)
        att_copy(unit, ATT_RIGHT).start()
        att_copy(unit, ATT_LEFT).start()

    def project(image, side, slots):
        parts = [
            jnp.dot(attended[image * SLOTS + slot], wo[side, slot], preferred_element_type=F32)
            for slot in slots
        ]
        return parts[0] if len(parts) == 1 else parts[0] + parts[1]

    def route_on(group, hop):
        if hop != 0:
            first_copy(group, hop).wait_recv()
        for core in range(2):
            @pl.when(gy == core)
            def _():
                for step in (2, 1, 3):
                    last_copy(group, hop, step, core).start()

                @pl.when(group == gy)
                def _():
                    stay_copy(group, hop, core).start()

                @pl.when(group != gy)
                def _():
                    last_copy(group, hop, 0, core).start()

    def finish(held_image):
        part_copy(held_image).wait_recv()
        rows = pl.ds(pl.multiple_of(lax.rem(held_image, 2) * PATCHES, PATCHES), PATCHES)
        layer[rows, :] = (
            x_half[lax.div(held_image, 2), rows, :].astype(F32)
            + (mine[held_image].astype(F32) + other[held_image].astype(F32))
        ).astype(BF16)

    def prepare(group):
        finish(2 * group)
        place = lax.broadcasted_iota(jnp.int32, (RING * CAP, 1), 0)
        places = target[group][0:1, :]
        for step in range(RING):
            rank = plane(lax.rem(first_at + step, RING), place >> 6)
            picks[step] = jnp.where(
                rank * CAP + (place & (CAP - 1)) == places, 1.0, 0.0
            ).astype(BF16)

    def route(group):
        finish(2 * group + 1)
        for step in (2, 1, 3, 0):
            picked = jnp.dot(picks[step], layer[...], preferred_element_type=F32).astype(BF16)
            picked = picked.reshape(RING, CAP, WIDE)
            if step == 0:
                for to in range(RING):
                    middle[group, to, first_at] = picked[to]
                route_on(group, 0)
            else:
                outgoing[group, step - 1] = picked
                first_copy(group, step).start()

    def towards_opposite(unit):
        two[unit] = product(unit, OPP).astype(BF16)
        sum_copy(unit, TWO_RIGHT).start()
        sum_copy(unit, TWO_LEFT).start()

    normalize(0)
    sum_copy(first_unit, TWO_RIGHT).wait_recv()
    to_right[first_unit, LOW, :] = (
        to_right[first_unit, LOW, :].astype(F32) + from_two_left[first_unit].astype(F32)
    ).astype(BF16)
    sum_copy(first_unit, RIGHT_LOW).start()
    sum_copy(first_unit, TWO_LEFT).wait_recv()
    to_left[first_unit, HIGH, :] = (
        to_left[first_unit, HIGH, :].astype(F32) + from_two_right[first_unit].astype(F32)
    ).astype(BF16)
    sum_copy(first_unit, LEFT_HIGH).start()
    wait_weights(OPP, 1)

    @pl.when(gy == 0)
    def _():
        towards_opposite(1)

    normalize(1)

    @pl.when(gy == 1)
    def _():
        norm_copy(0).wait_recv()
        towards_opposite(0)

    row = lax.broadcasted_iota(jnp.int32, (8, 2 * PATCHES), 1)
    places = jnp.full((8, 2 * PATCHES), RANKS * CAP, jnp.int32)
    for image in range(2):
        begin = image * PATCHES
        for piece in range(8):
            stop = begin + counts_ref[image, piece]
            places = jnp.where(
                (row >= begin) & (row < stop), dest_ref[image, piece] * CAP + row - begin, places
            )
            begin = stop
    target[gy] = places
    target_copy = remote(target.at[gy], target.at[gy], target_send, target_recv, sibling)
    target_copy.start()
    cross_copy = remote(
        x_hbm.at[:, pl.ds(pl.multiple_of((1 - gy) * WIDE, WIDE), WIDE)],
        x_half.at[gy], half_send, half_recv, sibling,
    )
    cross_copy.start()
    half_copy.start()
    for copy in wo_copies():
        copy.start()

    def turn(step, carry):
        def back(count):
            at_turn = lax.rem(step + UNITS - count, UNITS)
            late = lax.div(at_turn, 2 * SLOTS + 1)
            shifted = lax.rem(at_turn + 2 * SLOTS, 2 * SLOTS + 1)
            return (1 - gy) * at_turn + gy * (late * at_turn + (1 - late) * shifted)

        @pl.when((step >= 2) & (step <= UNITS))
        def _():
            unit = back(1)

            @pl.when(step <= SLOTS)
            def _():
                wait_weights(RIGHT, lax.rem(step + 2, SLOTS))
                wait_weights(LEFT, lax.rem(step + 2, SLOTS))

            mine_right = product(unit, RIGHT)
            to_right[unit, HIGH, :] = mine_right[HALF:, :].astype(BF16)
            sum_copy(unit, RIGHT_HIGH).start()
            sum_copy(unit, TWO_RIGHT).wait_recv()
            to_right[unit, LOW, :] = (
                mine_right[:HALF, :] + from_two_left[unit].astype(F32)
            ).astype(BF16)
            sum_copy(unit, RIGHT_LOW).start()
            mine_left = product(unit, LEFT)
            to_left[unit, LOW, :] = mine_left[:HALF, :].astype(BF16)
            sum_copy(unit, LEFT_LOW).start()
            sum_copy(unit, TWO_LEFT).wait_recv()
            to_left[unit, HIGH, :] = (
                mine_left[HALF:, :] + from_two_right[unit].astype(F32)
            ).astype(BF16)
            sum_copy(unit, LEFT_HIGH).start()

        @pl.when((step >= 1) & (step <= UNITS - 2))
        def _():
            unit = back(-1)
            image = lax.div(unit, SLOTS)

            @pl.when((lax.rem(unit, SLOTS) == 0) & (lax.div(image, 2) != gy))
            def _():
                norm_copy(lax.rem(image, 2)).wait_recv()

            @pl.when(step == 1)
            def _():
                wait_weights(OPP, 2)

            towards_opposite(unit)

        @pl.when((step >= 2) & (step <= UNITS + 1))
        def _():
            unit = back(2)

            @pl.when(step < SLOTS + 2)
            def _():
                wait_weights(OWN, lax.rem(step + 1, SLOTS))

            attend(unit, step == 2)

        @pl.when((step >= 3) & (step <= UNITS + 2))
        def _():
            unit = back(3)
            att_copy(unit, ATT_RIGHT).wait_recv()
            att_copy(unit, PASS_RIGHT).start()
            att_copy(unit, ATT_LEFT).wait_recv()
            att_copy(unit, PASS_LEFT).start()

        @pl.when((step == 7) | (step == 10) | (step == 12) | (step == 16))
        def _():
            image = lax.div(step, 4) - 1

            @pl.when(step == 7)
            def _():
                for copy in wo_copies():
                    copy.wait()
                half_copy.wait()
                target_copy.wait()
                cross_copy.wait()

            def wait_slot(slot):
                att_copy(image * SLOTS + slot, PASS_RIGHT).wait_recv()
                att_copy(image * SLOTS + slot, PASS_LEFT).wait_recv()

            @pl.when(lax.rem(image, 2) == 1)
            def _():
                prepare(lax.div(image, 2))

            wait_slot(0)
            wait_slot(1)
            early = [project(image, side, (0, 1)) for side in range(2)]
            wait_slot(2)
            leaving[image] = (early[0] + project(image, 0, (2,))).astype(BF16)
            part_copy(image).start()
            mine[image] = (early[1] + project(image, 1, (2,))).astype(BF16)

        @pl.when((step == 10) | (step == 16))
        def _():
            route(lax.div(step, 16))

        @pl.when((step == 12) | (step == 17))
        def _():
            for hop in (1, 3, 2):
                route_on(lax.div(step, 17), hop)

        return carry

    lax.fori_loop(1, UNITS + 6, turn, 0)

    def drain(unit, carry):
        for kind in range(6):
            sum_copy(unit, kind).wait_send()
        for kind in range(4):
            att_copy(unit, kind).wait_send()
        return carry

    lax.fori_loop(0, UNITS, drain, 0)
    for copy in lead_copies:
        copy.wait_send()
    for image in range(2):
        norm_copy(image).wait_send()
    for image in range(IMAGES):
        part_copy(image).wait_send()
    for group in range(2):
        for step in range(1, RING):
            first_copy(group, step).wait_send()
        for hop in range(RING):
            for step in range(1, RING):
                last_copy(group, hop, step, group).wait_send()
                last_copy(group, hop, step, group).wait_recv()

            @pl.when(group != gy)
            def _():
                last_copy(group, hop, 0, group).wait_send()
                last_copy(group, hop, 0, group).wait_recv()

            @pl.when(group == gy)
            def _():
                stay_copy(group, hop, group).wait()


def on_device(x_in, ln_gain, w_qkv, q_gain, k_gain, w_out, counts, dest):
    any_spec = pl.BlockSpec(memory_space=pl.ANY)
    dma = pltpu.SemaphoreType.DMA
    routed = pl.pallas_call(
        kernel,
        out_shape=pltpu.VMEM((RING, RING, CAP, BLOCK), BF16),
        in_specs=[any_spec] * 8,
        out_specs=any_spec,
        scratch_shapes=[
            pltpu.VMEM((2 * PATCHES, BLOCK), BF16),
            pltpu.VMEM((BLOCK,), F32),
            pltpu.VMEM((1, 128), F32),
            pltpu.VMEM((1, 128), F32),
            pltpu.SMEM((2, 8), jnp.int32),
            pltpu.SMEM((2, 8), jnp.int32),
            pltpu.VMEM((2, 2 * PATCHES, WIDE), BF16),
            pltpu.VMEM((IMAGES, PATCHES, BLOCK), BF16),
            pltpu.VMEM((4, SLOTS, BLOCK, GROUP), BF16),
            pltpu.VMEM((2, SLOTS, 4 * 128, WIDE), BF16),
            pltpu.VMEM((UNITS, PATCHES, GROUP), BF16),
            pltpu.VMEM((UNITS, PATCHES, GROUP), BF16),
            pltpu.VMEM((UNITS, PATCHES, GROUP), BF16),
            pltpu.VMEM((UNITS, HALF, GROUP), BF16),
            pltpu.VMEM((UNITS, HALF, GROUP), BF16),
            pltpu.VMEM((UNITS, PATCHES, GROUP), BF16),
            pltpu.VMEM((UNITS, PATCHES, GROUP), BF16),
            pltpu.VMEM((UNITS, PATCHES, 4 * 128), BF16),
            pltpu.VMEM((PATCHES, GROUP), F32),
            pltpu.VMEM((PATCHES + 16, BLOCK), BF16),
            pltpu.VMEM((PATCHES, 128), F32),
            pltpu.VMEM((4, 8, GROUP), F32),
            pltpu.VMEM((3, 8, GROUP), F32),
            pltpu.VMEM((IMAGES, PATCHES, WIDE), BF16),
            pltpu.VMEM((IMAGES, PATCHES, WIDE), BF16),
            pltpu.VMEM((IMAGES, PATCHES, WIDE), BF16),
            pltpu.VMEM((2 * PATCHES, WIDE), BF16),
            pltpu.VMEM((RING, RING * CAP, 2 * PATCHES), BF16),
            pltpu.VMEM((2, RING - 1, RING, CAP, WIDE), BF16),
            pltpu.VMEM((2, RING, RING, CAP, WIDE), BF16),
            pltpu.VMEM((2, 8, 2 * PATCHES), jnp.int32),
            pltpu.VMEM((2, 8, PATCHES), F32),
            pltpu.VMEM((2, 3, 8, PATCHES), F32),
            dma((2,)),
            dma((5,)),
            dma(()),
            dma((4, SLOTS, 3)),
            dma((2, SLOTS, 4)),
            dma(()),
            dma(()),
            dma(()),
            dma(()),
            dma((2, 3)),
            dma((2, 3)),
            dma((3,)),
            dma((3,)),
            dma((2,)),
            dma((2,)),
            dma((UNITS, 6)),
            dma((UNITS, 6)),
            dma((UNITS, 4)),
            dma((UNITS, 4)),
            dma((IMAGES,)),
            dma((IMAGES,)),
            dma((2, RING - 1)),
            dma((2, RING - 1)),
            dma((2, RING, RING)),
            dma((2, RING, RING)),
            dma((RING,)),
        ],
        compiler_params=pltpu.CompilerParams(
            collective_id=0, has_side_effects=True, vmem_limit_bytes=58 * 2**20
        ),
        cost_estimate=pl.CostEstimate(
            flops=20 * 10**9, bytes_accessed=25 * 10**6, transcendentals=10**6
        ),
        name="layer",
    )(
        x_in.reshape(2 * PATCHES, BLOCK),
        ln_gain,
        jnp.transpose(w_qkv, (1, 2, 0, 3)),
        q_gain.reshape(1, 128),
        k_gain.reshape(1, 128),
        w_out.reshape(BLOCK, BLOCK),
        counts,
        dest,
    )
    return routed.reshape(1, 1, RANKS, 1, CAP, BLOCK)


def solution(mesh):
    in_specs = (
        P(("gy", "gz"), None, "gx"),
        P("gx"),
        P("gx", "gy", None, None),
        P(),
        P(),
        P("gy", None, "gx"),
        P(("gy", "gz"), None),
        P(("gy", "gz"), None),
    )
    out_specs = P("gy", "gz", None, None, None, "gx")
    return jax.shard_map(
        on_device, mesh=mesh, in_specs=in_specs, out_specs=out_specs, check_vma=False
    )
```

time: 151 us -> 148 us (0.980)
  Pallas kernels: 149 us -> 146 us
    pallas_call x1, Pallas kernels: 149 us -> 146 us  [on_device(): pl.pallas_call(kernel, out_shape=pltpu.VMEM((RING, RING, CAP, BLOCK), BF1...]
where the time goes in v3:
time: 148 us
  Pallas kernels  146 us (99%)
  local copies, waits for them, and re-layouts  1.67 us (1%)
    pallas_call x1, Pallas kernels, on_device(): pl.pallas_call(kernel, out_shape=pltpu.VMEM((RING, RING, CAP, BLOCK), BF1...  146 us

profile of v3, /device:TPU:1, one launch (start us, length us, event | category | flops | bytes accessed | tf_op | source)
XLA Modules:
  0.0 148.0 jit_solution(3828413481816845789)
XLA Ops:
  0.0 146.3 %layer.1 = bf16[4,4,64,1536]{3,2,1,0:T(8,128)(2,1)S(1)} custom-call(bf16[512,1536]{1,0:T(8,128)(2,1)} %bitcast.11, f32[1536]{0:T(1024)} %gain_hbm.1, bf16[12,3,1536,128]{3,2,1,0:T(8,128)(2,1)} %bitcast.9, f32[1,128]{1,0:T(1,128)} %bitcast.12, f32[1,128]{1,0:T(1,128)} %bitcast.13, bf16[1536,1536]{1,0:T(8,128)(2,1)} %bitcast.10, s32[2,8]{1,0:T(2,128)} %counts_hbm.1, ...), custom_call_target="tpu_custom_call" | custom-call | flops 20000000000 | bytes 25000000 | tf_op jit(solution)/shard_map/layer/pallas_call | solution.py:593
  146.3 1.7 %copy.11 = bf16[1,1,16,1,64,1536]{5,4,3,2,1,0:T(8,128)(2,1)} copy(bf16[1,1,16,1,64,1536]{5,4,3,2,1,0:T(8,128)(2,1)S(1)} %bitcast.8) | data formatting | bytes 6291456

commit v4 on v3

--- a/solution.py
+++ b/solution.py
@@ -269,11 +269,12 @@
             leaving.at[image], other.at[image], part_send.at[image], part_recv.at[image], sibling
         )
 
-    def first_copy(group, step):
+    def first_copy(group, hop, step):
+        to = lax.rem(last_at + step, RING)
         return remote(
-            outgoing.at[group, step - 1], middle.at[group, :, first_at],
-            first_send.at[group, step - 1], first_recv.at[group, step - 1],
-            (gx, gy, on_first(step)),
+            outgoing.at[group, hop - 1, to], middle.at[group, to, first_at],
+            first_send.at[group, hop - 1, step], first_recv.at[group, hop - 1, step],
+            (gx, gy, on_first(hop)),
         )
 
     columns = {core: pl.ds(core * WIDE, WIDE) for core in range(2)}
@@ -349,22 +350,29 @@
         ]
         return parts[0] if len(parts) == 1 else parts[0] + parts[1]
 
-    def route_on(group, hop):
-        if hop != 0:
-            first_copy(group, hop).wait_recv()
+    def send_last(group, hop, step):
         for core in range(2):
             @pl.when(gy == core)
             def _():
-                for step in (2, 1, 3):
+                if step != 0:
                     last_copy(group, hop, step, core).start()
-
-                @pl.when(group == gy)
-                def _():
-                    stay_copy(group, hop, core).start()
-
-                @pl.when(group != gy)
-                def _():
-                    last_copy(group, hop, 0, core).start()
+                else:
+                    @pl.when(group == gy)
+                    def _():
+                        stay_copy(group, hop, core).start()
+
+                    @pl.when(group != gy)
+                    def _():
+                        last_copy(group, hop, 0, core).start()
+
+    def route_on(group):
+        for hop in (1, 3, 2):
+            for step in (2, 1, 3):
+                first_copy(group, hop, step).wait_recv()
+                send_last(group, hop, step)
+        for hop in range(1, RING):
+            first_copy(group, hop, 0).wait_recv()
+            send_last(group, hop, 0)
 
     def finish(held_image):
         part_copy(held_image).wait_recv()
@@ -386,16 +394,20 @@
 
     def route(group):
         finish(2 * group + 1)
-        for step in (2, 1, 3, 0):
+        for step in (1, 3, 2, 0):
             picked = jnp.dot(picks[step], layer[...], preferred_element_type=F32).astype(BF16)
             picked = picked.reshape(RING, CAP, WIDE)
             if step == 0:
                 for to in range(RING):
                     middle[group, to, first_at] = picked[to]
-                route_on(group, 0)
             else:
                 outgoing[group, step - 1] = picked
-                first_copy(group, step).start()
+                for on in (2, 1, 3):
+                    first_copy(group, step, on).start()
+        for step in (1, 3, 2):
+            first_copy(group, step, 0).start()
+        for on in (2, 1, 3, 0):
+            send_last(group, 0, on)
 
     def towards_opposite(unit):
         two[unit] = product(unit, OPP).astype(BF16)
@@ -455,6 +467,10 @@
             shifted = lax.rem(at_turn + 2 * SLOTS, 2 * SLOTS + 1)
             return (1 - gy) * at_turn + gy * (late * at_turn + (1 - late) * shifted)
 
+        @pl.when((step == 9) | (step == 14))
+        def _():
+            prepare(lax.div(step, 14))
+
         @pl.when((step >= 2) & (step <= UNITS))
         def _():
             unit = back(1)
@@ -530,10 +546,6 @@
                 att_copy(image * SLOTS + slot, PASS_RIGHT).wait_recv()
                 att_copy(image * SLOTS + slot, PASS_LEFT).wait_recv()
 
-            @pl.when(lax.rem(image, 2) == 1)
-            def _():
-                prepare(lax.div(image, 2))
-
             wait_slot(0)
             wait_slot(1)
             early = [project(image, side, (0, 1)) for side in range(2)]
@@ -548,8 +560,7 @@
 
         @pl.when((step == 12) | (step == 17))
         def _():
-            for hop in (1, 3, 2):
-                route_on(lax.div(step, 17), hop)
+            route_on(lax.div(step, 17))
 
         return carry
 
@@ -570,8 +581,9 @@
     for image in range(IMAGES):
         part_copy(image).wait_send()
     for group in range(2):
-        for step in range(1, RING):
-            first_copy(group, step).wait_send()
+        for hop in range(1, RING):
+            for step in range(RING):
+                first_copy(group, hop, step).wait_send()
         for hop in range(RING):
             for step in range(1, RING):
                 last_copy(group, hop, step, group).wait_send()
@@ -650,8 +662,8 @@
             dma((UNITS, 4)),
             dma((IMAGES,)),
             dma((IMAGES,)),
-            dma((2, RING - 1)),
-            dma((2, RING - 1)),
+            dma((2, RING - 1, RING)),
+            dma((2, RING - 1, RING)),
             dma((2, RING, RING)),
             dma((2, RING, RING)),
             dma((RING,)),

time: 148 us -> 145 us (0.980)
  Pallas kernels: 146 us -> 143 us
    pallas_call x1, Pallas kernels: 146 us -> 143 us  [on_device(): pl.pallas_call(kernel, out_shape=pltpu.VMEM((RING, RING, CAP, BLOCK), BF1...]
where the time goes in v4:
time: 145 us; the launch traced here: 144 us
  Pallas kernels  143 us (99%)
  local copies, waits for them, and re-layouts  1.67 us (1%)
    pallas_call x1, Pallas kernels, on_device(): pl.pallas_call(kernel, out_shape=pltpu.VMEM((RING, RING, CAP, BLOCK), BF1...  143 us

profile of v4, /device:TPU:1, one launch (start us, length us, event | category | flops | bytes accessed | tf_op | source)
XLA Modules:
  0.0 144.3 jit_solution(7467186572358145505)
XLA Ops:
  0.0 142.7 %layer.1 = bf16[4,4,64,1536]{3,2,1,0:T(8,128)(2,1)S(1)} custom-call(bf16[512,1536]{1,0:T(8,128)(2,1)} %bitcast.11, f32[1536]{0:T(1024)} %gain_hbm.1, bf16[12,3,1536,128]{3,2,1,0:T(8,128)(2,1)} %bitcast.9, f32[1,128]{1,0:T(1,128)} %bitcast.12, f32[1,128]{1,0:T(1,128)} %bitcast.13, bf16[1536,1536]{1,0:T(8,128)(2,1)} %bitcast.10, s32[2,8]{1,0:T(2,128)} %counts_hbm.1, ...), custom_call_target="tpu_custom_call" | custom-call | flops 20000000000 | bytes 25000000 | tf_op jit(solution)/shard_map/layer/pallas_call | solution.py:605
  142.7 1.7 %copy.11 = bf16[1,1,16,1,64,1536]{5,4,3,2,1,0:T(8,128)(2,1)} copy(bf16[1,1,16,1,64,1536]{5,4,3,2,1,0:T(8,128)(2,1)S(1)} %bitcast.8) | data formatting | bytes 6291456

commit v5 on v4

--- a/solution.py
+++ b/solution.py
@@ -81,6 +81,13 @@
     def on_last(step):
         return plane(first_at, lax.rem(last_at + step, RING))
 
+    rows_of = [pl.ds(image * PATCHES, PATCHES) for image in range(2)]
+    x_copies = [
+        pltpu.make_async_copy(x_hbm.at[rows], x_ref.at[rows], x_sem.at[image])
+        for image, rows in enumerate(rows_of)
+    ]
+    x_copies[0].start()
+
     barrier = pltpu.get_barrier_semaphore()
     partners = [line[OPP], line[RIGHT], line[LEFT], sibling]
     for step in range(1, RING):
@@ -90,12 +97,6 @@
     for partner in partners:
         pl.semaphore_signal(barrier, inc=1, device_id=partner, device_id_type=MESH)
 
-    rows_of = [pl.ds(image * PATCHES, PATCHES) for image in range(2)]
-    x_copies = [
-        pltpu.make_async_copy(x_hbm.at[rows], x_ref.at[rows], x_sem.at[image])
-        for image, rows in enumerate(rows_of)
-    ]
-    x_copies[0].start()
     small_copies = [
         pltpu.make_async_copy(src, dst, small_sem.at[k])
         for k, (src, dst) in enumerate((
@@ -530,9 +531,9 @@
             att_copy(unit, ATT_LEFT).wait_recv()
             att_copy(unit, PASS_LEFT).start()
 
-        @pl.when((step == 7) | (step == 10) | (step == 12) | (step == 16))
-        def _():
-            image = lax.div(step, 4) - 1
+        @pl.when((step == 7) | (step == 10) | (step == 13) | (step == 16))
+        def _():
+            image = lax.div(step, 3) - 2
 
             @pl.when(step == 7)
             def _():

time: 145 us -> 145 us (level)
  no operation moved by 1% of the time
where the time goes in v5:
time: 145 us; the launch traced here: 144 us
  Pallas kernels  143 us (99%)
  local copies, waits for them, and re-layouts  1.67 us (1%)
    pallas_call x1, Pallas kernels, on_device(): pl.pallas_call(kernel, out_shape=pltpu.VMEM((RING, RING, CAP, BLOCK), BF1...  143 us

profile of v5, /device:TPU:1, one launch (start us, length us, event | category | flops | bytes accessed | tf_op | source)
XLA Modules:
  0.0 144.3 jit_solution(17785201637969665225)
XLA Ops:
  0.0 142.6 %layer.1 = bf16[4,4,64,1536]{3,2,1,0:T(8,128)(2,1)S(1)} custom-call(bf16[512,1536]{1,0:T(8,128)(2,1)} %bitcast.11, f32[1536]{0:T(1024)} %gain_hbm.1, bf16[12,3,1536,128]{3,2,1,0:T(8,128)(2,1)} %bitcast.9, f32[1,128]{1,0:T(1,128)} %bitcast.12, f32[1,128]{1,0:T(1,128)} %bitcast.13, bf16[1536,1536]{1,0:T(8,128)(2,1)} %bitcast.10, s32[2,8]{1,0:T(2,128)} %counts_hbm.1, ...), custom_call_target="tpu_custom_call" | custom-call | flops 20000000000 | bytes 25000000 | tf_op jit(solution)/shard_map/layer/pallas_call | solution.py:606
  142.6 1.7 %copy.11 = bf16[1,1,16,1,64,1536]{5,4,3,2,1,0:T(8,128)(2,1)} copy(bf16[1,1,16,1,64,1536]{5,4,3,2,1,0:T(8,128)(2,1)S(1)} %bitcast.8) | data formatting | bytes 6291456

commit v6 on v5

--- a/solution.py
+++ b/solution.py
@@ -392,17 +392,30 @@
             picks[step] = jnp.where(
                 rank * CAP + (place & (CAP - 1)) == places, 1.0, 0.0
             ).astype(BF16)
+            even = jnp.dot(
+                picks[step, :, 0:PATCHES], layer[0:PATCHES, :], preferred_element_type=F32
+            ).astype(BF16).reshape(RING, CAP, WIDE)
+            if step == 0:
+                for to in range(RING):
+                    middle[group, to, first_at] = even[to]
+            else:
+                outgoing[group, step - 1] = even
 
     def route(group):
         finish(2 * group + 1)
         for step in (1, 3, 2, 0):
-            picked = jnp.dot(picks[step], layer[...], preferred_element_type=F32).astype(BF16)
-            picked = picked.reshape(RING, CAP, WIDE)
+            picked = jnp.dot(
+                picks[step, :, PATCHES:], layer[PATCHES:, :], preferred_element_type=F32
+            ).reshape(RING, CAP, WIDE)
             if step == 0:
                 for to in range(RING):
-                    middle[group, to, first_at] = picked[to]
+                    middle[group, to, first_at] = (
+                        middle[group, to, first_at].astype(F32) + picked[to]
+                    ).astype(BF16)
             else:
-                outgoing[group, step - 1] = picked
+                outgoing[group, step - 1] = (
+                    outgoing[group, step - 1].astype(F32) + picked
+                ).astype(BF16)
                 for on in (2, 1, 3):
                     first_copy(group, step, on).start()
         for step in (1, 3, 2):

time: 145 us -> 146 us (level)
  no operation moved by 1% of the time
where the time goes in v6:
time: 146 us
  Pallas kernels  144 us (99%)
  local copies, waits for them, and re-layouts  1.67 us (1%)
    pallas_call x1, Pallas kernels, on_device(): pl.pallas_call(kernel, out_shape=pltpu.VMEM((RING, RING, CAP, BLOCK), BF1...  144 us

profile of v6, /device:TPU:1, one launch (start us, length us, event | category | flops | bytes accessed | tf_op | source)
XLA Modules:
  0.0 145.6 jit_solution(15974064023246308853)
XLA Ops:
  0.0 143.9 %layer.1 = bf16[4,4,64,1536]{3,2,1,0:T(8,128)(2,1)S(1)} custom-call(bf16[512,1536]{1,0:T(8,128)(2,1)} %bitcast.11, f32[1536]{0:T(1024)} %gain_hbm.1, bf16[12,3,1536,128]{3,2,1,0:T(8,128)(2,1)} %bitcast.9, f32[1,128]{1,0:T(1,128)} %bitcast.12, f32[1,128]{1,0:T(1,128)} %bitcast.13, bf16[1536,1536]{1,0:T(8,128)(2,1)} %bitcast.10, s32[2,8]{1,0:T(2,128)} %counts_hbm.1, ...), custom_call_target="tpu_custom_call" | custom-call | flops 20000000000 | bytes 25000000 | tf_op jit(solution)/shard_map/layer/pallas_call | solution.py:619
  143.9 1.7 %copy.11 = bf16[1,1,16,1,64,1536]{5,4,3,2,1,0:T(8,128)(2,1)} copy(bf16[1,1,16,1,64,1536]{5,4,3,2,1,0:T(8,128)(2,1)S(1)} %bitcast.8) | data formatting | bytes 6291456
